TPU v7x, 256 devices: a whole 4x4x8 slice. The times are simulated.
256 devices in a mesh: ep: 64 (over x, z, core), dp: 4 (over y).
Axes of the slice: x: 4, y: 4, z: 8, core: 2. Of those that a mesh axis runs over, the one named last changes fastest.
Arguments:
- tokens: bfloat16 [4096, 3584], P(('ep', 'dp')), may hold values from -6 to 6
- top_ids: int32 [4096, 8], P(('ep', 'dp')), may hold values from 0 to 127, all different within a row; in each aligned block of 16 rows (0 to 15, 16 to 31, ...) at most 2 rows name the same one
- gate_int: int32 [4096, 8], P(('ep', 'dp')), may hold values from 1 to 63
- replica_pick: int32 [4096, 8], P(('ep', 'dp')), may hold values 0 or 1
- plan: int32 [64], replicated, may hold values from 0 to 127, as said below
- gate_q: bfloat16 [128, 3584, 1024], P('ep', None, 'dp'), may hold values from -4 to 4
- gate_scale: bfloat16 [128, 28, 8], P('ep', None, 'dp'), may hold values from 0.008300781 to 0.033203125
- up_q: bfloat16 [128, 3584, 1024], P('ep', None, 'dp'), may hold values from -4 to 4
- up_scale: bfloat16 [128, 28, 8], P('ep', None, 'dp'), may hold values from 0.008300781 to 0.033203125
- down_q: bfloat16 [128, 1024, 3584], P('ep', 'dp'), may hold values from -4 to 4
- down_scale: bfloat16 [128, 8, 28], P('ep', 'dp'), may hold values from 0.015625 to 0.0625
Outputs:
- combined: bfloat16 [4096, 3584], P(('ep', 'dp'))
- slot_fill: float32 [64, 3, 256], P('ep')
- moved_down: bfloat16 [64, 1024, 3584], P('ep', 'dp')
- moved_down_scale: bfloat16 [64, 8, 28], P('ep', 'dp')
Inputs may be any that keep to these rules, and one draw needn't show every extreme that they name: `top_ids`: no expert is named by more than 2 of the 16 rows of one device, and some expert reaches 2; the 8 experts of a row differ. `plan`: entry r is one of the 2 experts of ep index (r + m // 2) mod m, with m = 64.
All inputs are finite; a program needn't handle non-finite values. No bound on the sum of `replica_pick` on one device may be relied on, other than what follows from the above.
Results may differ from a plain program's by a relative error of at most 0.015.
Values may be sent and summed in bfloat16 or wider, within the bound.
A program may use at most 128 MiB of HBM per device.

v0:
```python
import jax
import jax.numpy as jnp
from jax import lax
from jax.sharding import PartitionSpec as P

EXP_DEV = 2


def passed_along(block, axis, distance):
    devices = range(lax.axis_size(axis))
    route = [((i - distance) % len(devices), i) for i in devices]
    return lax.ppermute(block, axis, route)


def dequant(quant, scales):
    leading = quant.shape[:-2]
    rows_q = quant.shape[-2]
    cols_q = quant.shape[-1]
    row_blocks = scales.shape[-2]
    col_blocks = scales.shape[-1]
    widened = jnp.repeat(scales, cols_q // col_blocks, axis=-1).astype(jnp.float32)
    blocked = quant.reshape(leading + (row_blocks, rows_q // row_blocks, cols_q)).astype(
        jnp.float32
    )
    scaled = blocked * jnp.expand_dims(widened, -2)
    return scaled.astype(jnp.bfloat16).reshape(leading + (rows_q, cols_q))


def choose(array, index):
    return lax.dynamic_index_in_dim(array, index, 0, keepdims=False)


def build_routes(row_block, expert_ids, gate_ints, pick_flags, plan, n_ep, depth):
    local_rows, top_count = expert_ids.shape
    slot_count = EXP_DEV + 1
    half_ep = n_ep // 2
    home_ep = expert_ids // EXP_DEV
    partner = (home_ep + half_ep) % n_ep
    peer_plan = jnp.sum(
        jnp.where(partner[..., None] == jnp.arange(n_ep, dtype=jnp.int32), plan, 0), axis=-1
    )
    to_copy = (peer_plan == expert_ids) & (pick_flags == 1)
    target = jnp.where(to_copy, partner, home_ep)
    slot_idx = jnp.where(to_copy, EXP_DEV, expert_ids % EXP_DEV)
    slot_key = (target * slot_count + slot_idx).reshape(-1)
    serial = jnp.arange(slot_key.shape[0], dtype=jnp.int32)
    earlier = (slot_key[:, None] == slot_key[None, :]) & (serial[None, :] < serial[:, None])
    rank_in = jnp.sum(earlier.astype(jnp.int32), axis=1)
    position = slot_key * depth + rank_in
    capacity = n_ep * slot_count * depth
    onehot = (position[:, None] == jnp.arange(capacity, dtype=jnp.int32)[None, :]).reshape(
        local_rows, top_count, capacity
    )
    chosen = jnp.sum(onehot.astype(jnp.float32), axis=1).astype(jnp.bfloat16)
    outgoing = jnp.einsum(
        "rp,rd->pd", chosen, row_block, preferred_element_type=jnp.float32
    ).astype(jnp.bfloat16)
    outgoing = outgoing.reshape(n_ep, slot_count, depth, row_block.shape[1])
    weights = gate_ints.astype(jnp.float32)
    weights = weights / jnp.sum(weights, axis=-1, keepdims=True)
    mixing = jnp.sum(onehot.astype(jnp.float32) * weights[..., None], axis=1)
    tallies = jnp.sum(
        (slot_key[:, None] == jnp.arange(n_ep * slot_count, dtype=jnp.int32)[None, :]).astype(
            jnp.int32
        ),
        axis=0,
    )
    return (outgoing, tallies.reshape(n_ep, slot_count), mixing)


def apply_slots(block, slot_weights):
    leading = block.shape[0]
    results = []
    for index in range(len(slot_weights)):
        gate_w, up_w, down_w = slot_weights[index]
        flat_rows = block[:, index].reshape(-1, block.shape[-1])
        gate_v = jnp.dot(flat_rows, gate_w, preferred_element_type=jnp.float32)
        up_v = jnp.dot(flat_rows, up_w, preferred_element_type=jnp.float32)
        hidden = (jax.nn.silu(gate_v) * up_v).astype(jnp.bfloat16)
        output = jnp.dot(hidden, down_w, preferred_element_type=jnp.float32)
        results.append(output.reshape(leading, block.shape[2], down_w.shape[1]))
    return jnp.stack(results, axis=1)


def per_device(
    tokens,
    top_ids,
    gate_int,
    replica_pick,
    plan,
    gate_q,
    gate_scale,
    up_q,
    up_scale,
    down_q,
    down_scale,
):
    n_ep = lax.axis_size("ep")
    n_dp = lax.axis_size("dp")
    half_ep = n_ep // 2
    ep_index = lax.axis_index("ep")
    local_rows, top_count = top_ids.shape
    width = tokens.shape[1]
    slot_count = EXP_DEV + 1
    depth = max(2, local_rows * top_count // (EXP_DEV * n_ep))
    receiver = (ep_index + half_ep) % n_ep
    wanted = plan[receiver] - ep_index * EXP_DEV
    copies = passed_along(
        (
            choose(gate_q, wanted),
            choose(gate_scale, wanted),
            choose(up_q, wanted),
            choose(up_scale, wanted),
            choose(down_q, wanted),
            choose(down_scale, wanted),
        ),
        "ep",
        half_ep,
    )
    gate_local = dequant(gate_q, gate_scale)
    up_local = dequant(up_q, up_scale)
    down_local = dequant(down_q, down_scale)
    slot_weights = [
        (gate_local[index], up_local[index], down_local[index]) for index in range(EXP_DEV)
    ]
    slot_weights.append(
        (
            dequant(copies[0], copies[1]),
            dequant(copies[2], copies[3]),
            dequant(copies[4], copies[5]),
        )
    )
    outgoing, tallies, mixing = build_routes(
        tokens, top_ids, gate_int, replica_pick, plan, n_ep, depth
    )
    arrived, arrived_counts = (
        lax.all_to_all(outgoing, "ep", split_axis=0, concat_axis=0, tiled=True),
        lax.all_to_all(tallies.astype(jnp.bfloat16), "ep", split_axis=0, concat_axis=0, tiled=True),
    )
    gathered, gathered_counts = (
        lax.all_gather(arrived, "dp", axis=0, tiled=True),
        lax.all_gather(arrived_counts, "dp", axis=0, tiled=True),
    )
    summed = lax.psum_scatter(
        apply_slots(gathered, slot_weights).astype(jnp.bfloat16),
        "dp",
        scatter_dimension=0,
        tiled=True,
    )
    column_counts = gathered_counts.reshape(n_dp, n_ep, slot_count)
    returned = lax.all_to_all(summed, "ep", split_axis=0, concat_axis=0, tiled=True)
    combined = jnp.dot(
        mixing, returned.reshape(-1, width).astype(jnp.float32), precision=lax.Precision.HIGHEST
    )
    slot_fill = column_counts.astype(jnp.float32).transpose(2, 1, 0).reshape(
        1, slot_count, n_ep * n_dp
    ) / jnp.float32(depth)
    return (combined.astype(jnp.bfloat16), slot_fill, copies[4][None], copies[5][None])


def solution(mesh):
    return jax.shard_map(
        per_device,
        mesh=mesh,
        in_specs=(
            P(("ep", "dp"), None),
            P(("ep", "dp"), None),
            P(("ep", "dp"), None),
            P(("ep", "dp"), None),
            P(),
            P("ep", None, "dp"),
            P("ep", None, "dp"),
            P("ep", None, "dp"),
            P("ep", None, "dp"),
            P("ep", "dp", None),
            P("ep", "dp", None),
        ),
        out_specs=(
            P(("ep", "dp"), None),
            P("ep", None, None),
            P("ep", "dp", None),
            P("ep", "dp", None),
        ),
        check_vma=False,
    )
```

profile of v0, /device:TPU:2, one launch (start us, length us, event | category | flops | bytes accessed | tf_op | source)
XLA Modules:
  0.0 489.1 jit_solution(16887026952803035932)
XLA Ops:
  12.8 2.5 reshape.166
  15.3 76.4 %all_to_all.19 = bf16[64,3,2,3584]{3,2,1,0:T(2,128)(2,1)} all-to-all(bf16[64,3,2,3584]{3,2,1,0:T(2,128)(2,1)} %reshape.166), channel_id=1, replica_groups=mesh['ep'=64,'dp'=4] {'ep'}, dimensions={0} | all-to-all | bytes 5505024 | tf_op jit(solution)/shard_map/all_to_all | solution.py:137
  93.1 3.0 dynamic-slice_bitcast_fusion.2
  96.1 2.3 collective-permute-start
  101.1 2.3 collective-permute-start.2
  106.0 2.3 collective-permute-start.4
  109.1 3.5 fusion.2
  121.1 19.7 %collective-permute-done.1 = bf16[28,2]{0,1:T(2,128)(2,1)S(1)} collective-permute-done((bf16[28,2]{0,1:T(2,128)(2,1)S(1)}, bf16[28,2]{0,1:T(2,128)(2,1)S(1)}, u32[]{:S(2)}, u32[]{:S(2)}) %collective-permute-start.1) | collective-permute-done | bytes 144 | tf_op jit(solution)/shard_map/ppermute | solution.py:12
  140.8 2.3 collective-permute-start.5
  143.4 36.8 %collective-permute-done.3 = bf16[28,2]{0,1:T(2,128)(2,1)S(1)} collective-permute-done((bf16[28,2]{0,1:T(2,128)(2,1)S(1)}, bf16[28,2]{0,1:T(2,128)(2,1)S(1)}, u32[]{:S(2)}, u32[]{:S(2)}) %collective-permute-start.3) | collective-permute-done | bytes 144 | tf_op jit(solution)/shard_map/ppermute | solution.py:12
  180.4 39.1 %collective-permute-done.5 = bf16[2,28]{1,0:T(2,128)(2,1)S(1)} collective-permute-done((bf16[2,28]{1,0:T(2,128)(2,1)S(1)}, bf16[2,28]{1,0:T(2,128)(2,1)S(1)}, u32[]{:S(2)}, u32[]{:S(2)}) %collective-permute-start.5) | collective-permute-done | bytes 144 | tf_op jit(solution)/shard_map/ppermute | solution.py:12
  219.6 3.1 fusion.8
  222.7 3.1 fusion.7
  225.7 3.0 fusion.6
  228.8 10.3 %fusion.25 = (bf16[256,1,2,3584]{3,2,1,0:T(2,128)(2,1)}, bf16[256,1,2,3584]{3,2,1,0:T(2,128)(2,1)}, bf16[256,1,2,3584]{3,2,1,0:T(2,128)(2,1)}) fusion(bf16[256,3,2,3584]{3,2,1,0:T(2,128)(2,1)} %all-gather.3.cloned.1.call-done), kind=kLoop, calls=%fused_computation.70 | loop fusion | bytes 22020096 | tf_op jit(solution)/shard_map/slice | solution.py:76
  239.0 8.4 %reshape_squeeze.11 = bf16[512,3584]{1,0:T(8,128)(2,1)} reshape(bf16[256,1,2,3584]{3,2,1,0:T(2,128)(2,1)} %get-tuple-element.27) | data formatting | bytes 7340032 | tf_op jit(solution)/shard_map/reshape;squeeze | solution.py:76
  247.4 3.9 fusion.31
  252.9 8.4 %reshape_squeeze.9 = bf16[512,3584]{1,0:T(8,128)(2,1)} reshape(bf16[256,1,2,3584]{3,2,1,0:T(2,128)(2,1)} %get-tuple-element.26) | data formatting | bytes 7340032 | tf_op jit(solution)/shard_map/reshape;squeeze | solution.py:76
  261.3 3.9 fusion.29
  266.7 8.4 %reshape_squeeze.10 = bf16[512,3584]{1,0:T(8,128)(2,1)} reshape(bf16[256,1,2,3584]{3,2,1,0:T(2,128)(2,1)} %get-tuple-element.28) | data formatting | bytes 7340032 | tf_op jit(solution)/shard_map/reshape;squeeze | solution.py:76
  275.1 3.9 fusion.30
  280.6 2.7 fusion.5
  285.6 5.1 %pad_maximum_fusion = bf16[256,3,2,3584]{3,0,2,1:T(8,128)(2,1)} fusion(bf16[256,1,2,3584]{3,0,2,1:T(8,128)(2,1)S(1)} %fusion.5, bf16[256,1,2,3584]{3,0,2,1:T(8,128)(2,1)S(1)} %fusion.4, bf16[256,1,2,3584]{3,0,2,1:T(8,128)(2,1)S(1)} %fusion.3), kind=kLoop, calls=%fused_computation | loop fusion | flops 11010048 | bytes 22020096 | tf_op jit(solution)/shard_map/stack | solution.py:82
  291.7 6.2 %all-to-all-start.2 = ((bf16[64,1,3]{2,1,0:T(2,128)(2,1)}), bf16[64,1,3]{2,1,0:T(2,128)(2,1)S(1)}, u32[]{:S(2)}, u32[]{:S(2)}) async-start(bf16[64,1,3]{2,1,0:T(2,128)(2,1)} %convert_element_type.211), calls=%async_computation.3 | async-start | bytes 65536 | tf_op jit(solution)/shard_map/all_to_all | solution.py:138
  297.9 94.5 %reduce-scatter.2.cloned.1.call-done = bf16[64,3,2,3584]{3,0,2,1:T(8,128)(2,1)} async-done(((bf16[256,3,2,3584]{3,0,2,1:T(8,128)(2,1)}), bf16[64,3,2,3584]{3,0,2,1:T(8,128)(2,1)}) %reduce-scatter.2.cloned.1.call-update) | async-done | bytes 2752528 | tf_op jit(solution)/shard_map/reduce_scatter | solution.py:144
  392.3 6.1 %copy.128 = bf16[64,3,2,3584]{3,2,1,0:T(2,128)(2,1)} copy(bf16[64,3,2,3584]{3,0,2,1:T(8,128)(2,1)} %reduce-scatter.2.cloned.1.call-done) | data formatting | bytes 5505024 | tf_op jit(solution)/shard_map/reduce_scatter | solution.py:144
  398.5 10.6 %all-to-all-start.1 = ((bf16[64,3,2,3584]{3,2,1,0:T(2,128)(2,1)}), bf16[64,3,2,3584]{3,2,1,0:T(2,128)(2,1)S(1)}, u32[]{:S(2)}, u32[]{:S(2)}) async-start(bf16[64,3,2,3584]{3,2,1,0:T(2,128)(2,1)} %copy.128), calls=%async_computation.2 | async-start | bytes 5505024 | tf_op jit(solution)/shard_map/all_to_all | solution.py:151
  409.0 12.0 %all-gather = bf16[256,1,3]{2,1,0:T(2,128)(2,1)S(1)} all-gather(bf16[64,1,3]{2,1,0:T(2,128)(2,1)S(1)} %all-to-all-done.2), channel_id=2, replica_groups=mesh['ep'=64,'dp'=4] {'dp'}, dimensions={0}, use_global_device_ids=true | all-gather | bytes 1920 | tf_op jit(solution)/shard_map/all_gather | solution.py:142
  422.1 50.7 %all-to-all-done.1 = bf16[64,3,2,3584]{3,2,1,0:T(2,128)(2,1)S(1)} async-done(((bf16[64,3,2,3584]{3,2,1,0:T(2,128)(2,1)}), bf16[64,3,2,3584]{3,2,1,0:T(2,128)(2,1)S(1)}, u32[]{:S(2)}, u32[]{:S(2)}) %all-to-all-start.1) | async-done | bytes 2752544 | tf_op jit(solution)/shard_map/all_to_all | solution.py:151
  472.8 2.5 reshape.170
  475.3 3.6 convolution_convert_fusion.4
  478.9 2.8 copy.146
  (108 shorter events, 30.6 us)
Async XLA Ops:
  7.2 4.8 copy-start
  7.2 221.6 %all-gather.3.cloned.1.call-start = ((), (), s32[]{:S(2)}) async-start(), calls=%async_computation.4 | async-start | bytes 13762560 | tf_op jit(solution)/shard_map/all_gather | solution.py:141
  15.3 76.5 %copy-start.16 = (s32[64]{0:T(128)S(1)}, s32[64]{0:T(128)}, u32[]{:S(2)}) copy-start(s32[64]{0:T(128)} %param.15) | copy-start | bytes 772
  91.7 6.7 %copy-start.14 = (bf16[2,28,2]{1,2,0:T(2,128)(2,1)S(1)}, bf16[2,28,2]{1,2,0:T(2,128)(2,1)}, u32[]{:S(2)}) copy-start(bf16[2,28,2]{1,2,0:T(2,128)(2,1)} %param.17) | copy-start | bytes 676
  91.8 300.6 %reduce-scatter.2.cloned.1.call-start = ((), (), s32[]{:S(2)}) async-start(), calls=%async_computation.5 | async-start | bytes 13762560 | tf_op jit(solution)/shard_map/reduce_scatter | solution.py:144
  93.1 6.6 %copy-start.2 = (bf16[2,3584,256]{2,1,0:T(8,128)(2,1)S(1)}, bf16[2,3584,256]{2,1,0:T(8,128)(2,1)}, u32[]{:S(2)}) copy-start(bf16[2,3584,256]{2,1,0:T(8,128)(2,1)} %param.18) | copy-start | bytes 11010052
  93.1 10.3 %copy-start.15 = (bf16[2,28,2]{1,2,0:T(2,128)(2,1)S(1)}, bf16[2,28,2]{1,2,0:T(2,128)(2,1)}, u32[]{:S(2)}) copy-start(bf16[2,28,2]{1,2,0:T(2,128)(2,1)} %param.19) | copy-start | bytes 676
  93.1 11.5 %copy-start.4 = (bf16[2,256,3584]{2,1,0:T(8,128)(2,1)S(1)}, bf16[2,256,3584]{2,1,0:T(8,128)(2,1)}, u32[]{:S(2)}) copy-start(bf16[2,256,3584]{2,1,0:T(8,128)(2,1)} %param.20) | copy-start | bytes 11010052
  96.1 123.4 %collective-permute-start = (bf16[3584,256]{1,0:T(8,128)(2,1)}, bf16[3584,256]{1,0:T(8,128)(2,1)}, u32[]{:S(2)}, u32[]{:S(2)}) collective-permute-start(bf16[3584,256]{1,0:T(8,128)(2,1)} %dynamic-slice_bitcast_fusion.2), channel_id=1, source_target_pairs={{128,0},{132,4},{136,8},{140,12},{144,16},{148,20},{152,24},{156,2... | collective-permute-start | bytes 5505032 | tf_op jit(solution)/shard_map/ppermute | solution.py:12
  98.4 10.5 %copy-start.13 = (bf16[2,2,28]{2,1,0:T(2,128)(2,1)S(1)}, bf16[2,2,28]{2,1,0:T(2,128)(2,1)}, u32[]{:S(2)}) copy-start(bf16[2,2,28]{2,1,0:T(2,128)(2,1)} %param.21) | copy-start | bytes 676
  98.4 42.4 %collective-permute-start.1 = (bf16[28,2]{0,1:T(2,128)(2,1)S(1)}, bf16[28,2]{0,1:T(2,128)(2,1)S(1)}, u32[]{:S(2)}, u32[]{:S(2)}) collective-permute-start(bf16[28,2]{0,1:T(2,128)(2,1)S(1)} %fusion.22), channel_id=1, source_target_pairs={{128,0},{132,4},{136,8},{140,12},{144,16},{148,20},{152,24},{156,2... | collective-permute-start | bytes 344 | tf_op jit(solution)/shard_map/ppermute | solution.py:12
  101.1 121.6 %collective-permute-start.2 = (bf16[3584,256]{1,0:T(8,128)(2,1)}, bf16[3584,256]{1,0:T(8,128)(2,1)}, u32[]{:S(2)}, u32[]{:S(2)}) collective-permute-start(bf16[3584,256]{1,0:T(8,128)(2,1)} %dynamic-slice_bitcast_fusion.1), channel_id=1, source_target_pairs={{128,0},{132,4},{136,8},{140,12},{144,16},{148,20},{152,24},{156,2... | collective-permute-start | bytes 5505032 | tf_op jit(solution)/shard_map/ppermute | solution.py:12
  103.4 76.8 %collective-permute-start.3 = (bf16[28,2]{0,1:T(2,128)(2,1)S(1)}, bf16[28,2]{0,1:T(2,128)(2,1)S(1)}, u32[]{:S(2)}, u32[]{:S(2)}) collective-permute-start(bf16[28,2]{0,1:T(2,128)(2,1)S(1)} %fusion.23), channel_id=1, source_target_pairs={{128,0},{132,4},{136,8},{140,12},{144,16},{148,20},{152,24},{156,2... | collective-permute-start | bytes 344 | tf_op jit(solution)/shard_map/ppermute | solution.py:12
  106.0 119.8 %collective-permute-start.4 = (bf16[256,3584]{1,0:T(8,128)(2,1)}, bf16[256,3584]{1,0:T(8,128)(2,1)}, u32[]{:S(2)}, u32[]{:S(2)}) collective-permute-start(bf16[256,3584]{1,0:T(8,128)(2,1)} %dynamic-slice_bitcast_fusion), channel_id=1, source_target_pairs={{128,0},{132,4},{136,8},{140,12},{144,16},{148,20},{152,24},{156,2... | collective-permute-start | bytes 5505032 | tf_op jit(solution)/shard_map/ppermute | solution.py:12
  109.1 3.6 copy-start.3
  112.6 2.0 copy-start.5
  140.8 78.6 %collective-permute-start.5 = (bf16[2,28]{1,0:T(2,128)(2,1)S(1)}, bf16[2,28]{1,0:T(2,128)(2,1)S(1)}, u32[]{:S(2)}, u32[]{:S(2)}) collective-permute-start(bf16[2,28]{1,0:T(2,128)(2,1)S(1)} %fusion.24), channel_id=1, source_target_pairs={{128,0},{132,4},{136,8},{140,12},{144,16},{148,20},{152,24},{156,2... | collective-permute-start | bytes 344 | tf_op jit(solution)/shard_map/ppermute | solution.py:12
  247.4 3.9 copy-start.8
  247.4 4.3 copy-start.12
  261.3 3.9 copy-start.9
  261.3 4.3 copy-start.11
  275.1 3.9 copy-start.7
  275.1 4.3 copy-start.10
  280.6 2.8 copy-start.6
  291.7 106.8 %all-to-all-start.2 = ((bf16[64,1,3]{2,1,0:T(2,128)(2,1)}), bf16[64,1,3]{2,1,0:T(2,128)(2,1)S(1)}, u32[]{:S(2)}, u32[]{:S(2)}) async-start(bf16[64,1,3]{2,1,0:T(2,128)(2,1)} %convert_element_type.211), calls=%async_computation.3 | async-start | bytes 65536 | tf_op jit(solution)/shard_map/all_to_all | solution.py:138
  398.5 74.3 %all-to-all-start.1 = ((bf16[64,3,2,3584]{3,2,1,0:T(2,128)(2,1)}), bf16[64,3,2,3584]{3,2,1,0:T(2,128)(2,1)S(1)}, u32[]{:S(2)}, u32[]{:S(2)}) async-start(bf16[64,3,2,3584]{3,2,1,0:T(2,128)(2,1)} %copy.128), calls=%async_computation.2 | async-start | bytes 5505024 | tf_op jit(solution)/shard_map/all_to_all | solution.py:151
  472.8 9.5 %copy-start.1 = (bf16[16,3584]{1,0:T(8,128)(2,1)S(1)}, bf16[16,3584]{1,0:T(8,128)(2,1)}, u32[]{:S(2)}) copy-start(bf16[16,3584]{1,0:T(8,128)(2,1)} %param.11) | copy-start | bytes 344068
Sparse Core Ops, SparseCore 0:
  91.9 105.9 all-gather.2
  290.9 101.3 reduce-scatter.1
where the time goes:
time: 493 us; the launch traced here: 489 us
  waiting for transfers between devices  241 us (49%)
  blocking collectives  88.4 us (18%)
  local copies, waits for them, and re-layouts  69 us (14%)
  starting transfers between devices  28.5 us (6%)
  matrix products  24.4 us (5%)
  other arithmetic  22.9 us (5%)
  between operations  15.2 us (3%)
    ppermute x6, waiting for transfers between devices, passed_along(): return lax.ppermute(block, axis, route)  95.6 us
    reduce_scatter x1, waiting for transfers between devices, per_device(): lax.psum_scatter(apply_slots(gathered, slot_weights).astype(jnp.bfloat16)...  94.5 us
    all_to_all x1, blocking collectives, per_device(): lax.all_to_all(outgoing, 'ep', split_axis=0, concat_axis=0, tiled=True)  76.4 us
    all_to_all x1, waiting for transfers between devices, per_device(): lax.all_to_all(summed, 'ep', split_axis=0, concat_axis=0, tiled=True)  50.7 us
    another operation x3, local copies, waits for them, and re-layouts, apply_slots(): flat_rows = block[:, index].reshape(-1, block.shape[-1])  25.2 us
    convert_element_type x6, other arithmetic, dequant(): return scaled.astype(jnp.bfloat16).reshape(leading + (rows_q, cols_q))  14.7 us
    all_gather x1, blocking collectives, per_device(): lax.all_gather(arrived_counts, 'dp', axis=0, tiled=True)  12 us
    ppermute x6, starting transfers between devices, passed_along(): return lax.ppermute(block, axis, route)  11.7 us
  transfers between devices with their start and end apart: 10, of which 5 were waited for; matrix products, arithmetic and copies ran while one was open for 7% of the time, Pallas kernels for 0%

commit v1 on v0

v1 whole, which is shorter than its diff:
```python
import functools

import jax
import jax.numpy as jnp
from jax import lax
from jax.experimental import pallas as pl
from jax.experimental.pallas import tpu as pltpu
from jax.sharding import PartitionSpec as P

NX, NZ, NC, NY = 4, 8, 2, 4
N_EP = NX * NZ * NC
ROWS = 16
TOPK = 8
EXP_DEV = 2
MOST = 2
CAP = N_EP * MOST
SLOTS = EXP_DEV * CAP
PLANE = N_EP * ROWS
D = 3584
FF = 256
BLOCK = 128
CW = 512
NCH = D // CW
RB = CW // BLOCK
F32 = jnp.float32
BF16 = jnp.bfloat16
MESH = pl.DeviceIdType.MESH


def kernel(
    tok, meta, gs, us, ds, gq_hbm, uq_hbm, dq_hbm,
    comb, cnt,
    dense, mg, xs, gq, uq, dq, accg, accu, hid, ryh, ryf, crecv, zrecv, xrecv,
    pack, unpack, wslot, cntbuf,
    w_sem, xi_s, xi_r, zi_s, zi_r, ci_s, ci_r, yi_s, yi_r, m_s, m_r,
    yo_s, yo_r, co_s, co_r, zo_s, zo_r, xo_s, xo_r, n_s, n_r,
):
    ep = lax.axis_index("ep")
    y = lax.axis_index("dp")
    c = ep % NC
    z = (ep // NC) % NZ
    x = ep // (NC * NZ)
    way = 1 - 2 * c
    y_up, y_dn, y_op = (y + 1) % NY, (y + NY - 1) % NY, (y + 2) % NY

    def zat(k):
        return (z + way * k + 2 * NZ) % NZ

    def xat(k):
        return (x + way * k + 2 * NX) % NX

    def at_x(k):
        return {"ep": (xat(k) * NZ + z) * NC + c, "dp": y}

    def at_z(k):
        return {"ep": (x * NZ + zat(k)) * NC + c, "dp": y}

    def at_y(to):
        return {"ep": ep, "dp": to}

    other = {"ep": (x * NZ + z) * NC + 1 - c, "dp": y}

    def remote(src, dst, ssem, rsem, dev):
        return pltpu.make_async_remote_copy(
            src_ref=src, dst_ref=dst, send_sem=ssem, recv_sem=rsem,
            device_id=dev, device_id_type=MESH,
        )

    def xblock(ref, core, zz, xx):
        return ref.at[pl.ds(core * NZ * NX + zz * NX + xx, 1)]

    def zblock(ref, core, zz):
        return ref.at[pl.ds(core * NZ * NX + zz * NX, NX)]

    def cblock(ref, core):
        return ref.at[pl.ds(core * NZ * NX, NZ * NX)]

    def g_x(ref, ss, rs, k, sent):
        off, hop = ((0, 1), (-1, 1), (0, -1))[k]
        if not sent:
            off = off - hop
        b = xblock(ref, c, z, xat(off))
        return remote(b, b, ss, rs, at_x(hop))

    def g_z(ref, ss, rs, k, sent):
        off, hop = ((0, 1), (-1, 1), (-2, 1), (-3, 1), (0, -1), (1, -1), (2, -1))[k]
        if not sent:
            off = off - hop
        b = zblock(ref, c, zat(off))
        return remote(b, b, ss, rs, at_z(hop))

    def g_c(ref, ss, rs, off):
        b = zblock(ref, c, zat(off))
        return remote(b, b, ss, rs, other)

    def g_c_all(ref, ss, rs, core):
        b = cblock(ref, core)
        return remote(b, b, ss, rs, other)

    def both(j, fn):
        fn(dense.at[j], (xi_s.at[j], xi_r.at[j], zi_s.at[j], zi_r.at[j], ci_s.at[j], ci_r.at[j]))

        @pl.when(j == 0)
        def _():
            fn(mg, (m_s.at[pl.ds(0, 3)], m_r.at[pl.ds(0, 3)], m_s.at[pl.ds(3, 7)],
                    m_r.at[pl.ds(3, 7)], m_s.at[10], m_r.at[10]))

    def x_start(j, k):
        both(j, lambda ref, q: g_x(ref, q[0].at[k], q[1].at[k], k, True).start())

    def x_recv(j, k):
        both(j, lambda ref, q: g_x(ref, q[0].at[k], q[1].at[k], k, False).wait_recv())

    def x_sent(j, k):
        both(j, lambda ref, q: g_x(ref, q[0].at[k], q[1].at[k], k, True).wait_send())

    def z_start(j, k):
        both(j, lambda ref, q: g_z(ref, q[2].at[k], q[3].at[k], k, True).start())

    def z_recv(j, k):
        both(j, lambda ref, q: g_z(ref, q[2].at[k], q[3].at[k], k, False).wait_recv())

    def z_sent(j, k):
        both(j, lambda ref, q: g_z(ref, q[2].at[k], q[3].at[k], k, True).wait_send())

    def c_start(j, off):
        both(j, lambda ref, q: g_c(ref, q[4], q[5], off).start())

    def c_recv(j):
        both(j, lambda ref, q: g_c_all(ref, q[4], q[5], 1 - c).wait_recv())

    def c_sent(j):
        both(j, lambda ref, q: g_c_all(ref, q[4], q[5], c).wait_send())

    half = SLOTS // 2

    def g_y(j, k, sent):
        if k < 2:
            to = (y_up, y_dn)[k]
            b = xs.at[j, y if sent else (y_dn, y_up)[k]]
        else:
            to = (y_up, y_dn)[k - 2]
            plane = (y_dn, y_up)[k - 2] if sent else y_op
            b = xs.at[j, plane, pl.ds((k - 2) * half, half)]
        return remote(b, b, yi_s.at[j, k], yi_r.at[j, k], at_y(to))

    barrier = pltpu.get_barrier_semaphore()
    partners = (at_x(1), at_x(-1), at_z(1), at_z(-1), other, at_y(y_up), at_y(y_dn), at_y(y_op))
    for dev in partners:
        pl.semaphore_signal(barrier, inc=1, device_id=dev, device_id_type=MESH)

    loads = [
        pltpu.make_async_copy(a, b, w_sem.at[i])
        for i, (a, b) in enumerate(((gq_hbm, gq), (uq_hbm, uq), (dq_hbm, dq)))
    ]
    for load in loads:
        load.start()
    own = c * NZ * NX + z * NX + x
    mg[own] = meta[...]
    for j in range(NCH):
        dense[j, own] = tok[:, j * CW:(j + 1) * CW]
    accg[...] = jnp.zeros_like(accg)
    accu[...] = jnp.zeros_like(accu)
    pl.semaphore_wait(barrier, len(partners))

    def x_begin(j, carry):
        x_start(j, 0)
        x_start(j, 2)
        return carry

    lax.fori_loop(0, NCH, x_begin, 0)

    def n_copy(k, sent):
        to = (y_up, y_dn, y_op)[k]
        b = cntbuf.at[y if sent else (y_dn, y_up, y_op)[k]]
        return remote(b, b, n_s.at[k], n_r.at[k], at_y(to))

    def routes():
        def rows_of(i):
            return mg[pl.ds(i * 8, 8)].reshape(BLOCK, BLOCK).astype(F32)

        lane = lax.broadcasted_iota(jnp.int32, (BLOCK, BLOCK), 1)
        row = lax.broadcasted_iota(jnp.int32, (BLOCK, BLOCK), 0)
        before = (lane < row).astype(BF16)
        first = (ep * EXP_DEV).astype(F32)
        slot0 = (ep * (EXP_DEV + 1)).astype(F32)
        fills = jnp.zeros((BLOCK, N_EP * NY), F32)
        sofar = jnp.zeros((1, BLOCK), F32)
        wsum = jnp.zeros((SLOTS, 1), F32)
        for i in range(PLANE // BLOCK):
            m = rows_of(i)
            gates = pltpu.roll(m, BLOCK - TOPK, 1)
            is_id = lane < TOPK
            den = jnp.sum(jnp.where(is_id, gates, 0.0), axis=1, keepdims=True)
            flags, weights = [], []
            for e in range(EXP_DEV):
                hit = is_id & (m == first + e)
                flags.append(jnp.sum(jnp.where(hit, 1.0, 0.0), axis=1, keepdims=True))
                weights.append(jnp.sum(jnp.where(hit, gates, 0.0), axis=1, keepdims=True) / den)
            flag = jnp.where(lane == 0, flags[0], jnp.where(lane == 1, flags[1], 0.0))
            place = jnp.dot(before, flag.astype(BF16), preferred_element_type=F32) + sofar
            sofar = sofar + jnp.sum(flag, axis=0, keepdims=True)
            spread = []
            for e in range(EXP_DEV):
                at = jnp.sum(jnp.where(lane == e, place, 0.0), axis=1, keepdims=True)
                at = at.astype(jnp.int32)
                spread.append(jnp.where((lane == at) & (flags[e] > 0.0), weights[e], 0.0))
            spread = jnp.concatenate(spread, axis=1)
            chosen = jnp.where(spread > 0.0, 1.0, 0.0)
            unpack[i * BLOCK:(i + 1) * BLOCK, :] = chosen.astype(BF16)
            turned = jnp.transpose(spread)
            pack[:, i * BLOCK:(i + 1) * BLOCK] = jnp.where(turned > 0.0, 1.0, 0.0).astype(BF16)
            wsum = wsum + jnp.sum(turned, axis=1, keepdims=True)
            keyed = (lane >= 2 * TOPK) & (lane < 3 * TOPK)
            tally = jnp.zeros((BLOCK, BLOCK), F32)
            for s in range(EXP_DEV + 1):
                n = jnp.sum(jnp.where(keyed & (m == slot0 + s), 1.0, 0.0), axis=1, keepdims=True)
                tally = tally + jnp.where(lane == s, n, 0.0)
            r = lax.broadcasted_iota(jnp.int32, (BLOCK, N_EP * NY), 0) + i * BLOCK
            col = lax.broadcasted_iota(jnp.int32, (BLOCK, N_EP * NY), 1)
            b = r >> 4
            source = (b & 3) * (NZ * NC) + ((b >> 2) & 7) * NC + (b >> 5)
            mine = (col == source * NY + y).astype(BF16)
            fills = fills + jnp.dot(jnp.transpose(tally).astype(BF16), mine, preferred_element_type=F32)
        wslot[...] = jnp.broadcast_to(wsum, (SLOTS, BLOCK))
        cntbuf[y] = fills[0:8]
        for k in range(3):
            n_copy(k, True).start()

    def weight(q, e, j, s):
        parts = []
        for i in range(RB):
            at = (j * RB + i) * 2
            row = jnp.where(
                lax.broadcasted_iota(jnp.int32, (1, FF), 1) < BLOCK, s[e, at], s[e, at + 1]
            )
            rows = q[e, pl.ds(pl.multiple_of(j * CW + i * BLOCK, BLOCK), BLOCK), :]
            parts.append((rows.astype(F32) * row).astype(BF16))
        return jnp.concatenate(parts, axis=0)

    def stage(t, late, fn):
        j = t - late

        @pl.when((j >= 0) & (j < NCH))
        def _():
            fn(j)

    def i1(j):
        x_recv(j, 0)
        x_start(j, 1)

    def i2(j):
        x_recv(j, 2)
        x_recv(j, 1)
        z_start(j, 0)
        z_start(j, 4)
        c_start(j, 0)

    def i3(j):
        z_recv(j, 0)
        z_start(j, 1)
        z_recv(j, 4)
        z_start(j, 5)
        c_start(j, -1)
        c_start(j, 1)

    def i4(j):
        z_recv(j, 1)
        z_start(j, 2)
        z_recv(j, 5)
        z_start(j, 6)
        c_start(j, -2)
        c_start(j, 2)

    def i5(j):
        z_recv(j, 2)
        z_start(j, 3)
        c_start(j, -3)
        z_recv(j, 6)
        c_start(j, 3)

    def i6(j):
        z_recv(j, 3)
        c_start(j, -4)

    def i7(j):
        c_recv(j)

        @pl.when(j == 0)
        def _():
            routes()

        full = dense[j].reshape(PLANE, CW)
        xs[j, y] = jnp.dot(pack[...], full, preferred_element_type=F32).astype(BF16)
        g_y(j, 0, True).start()
        g_y(j, 1, True).start()

    def i8(j):
        g_y(j, 0, False).wait_recv()
        g_y(j, 2, True).start()
        g_y(j, 1, False).wait_recv()
        g_y(j, 3, True).start()

    def i9(j):
        @pl.when(j == 0)
        def _():
            loads[0].wait()
            loads[1].wait()

        g_y(j, 2, False).wait_recv()
        g_y(j, 3, False).wait_recv()
        for e in range(EXP_DEV):
            rows = xs[j, :, e * CAP:(e + 1) * CAP, :].reshape(NY * CAP, CW)
            accg[e] += jnp.dot(rows, weight(gq, e, j, gs), preferred_element_type=F32)
            accu[e] += jnp.dot(rows, weight(uq, e, j, us), preferred_element_type=F32)

    def in_tick(t, carry):
        for late, fn in enumerate((i1, i2, i3, i4, i5, i6, i7, i8, i9)):
            stage(t, late, fn)
        return carry

    lax.fori_loop(0, NCH + 8, in_tick, 0)

    for e in range(EXP_DEV):
        v = accg[e]
        hid[e] = (v / (1.0 + jnp.exp(-v)) * accu[e]).astype(BF16)

    def in_done(j, carry):
        for k in range(3):
            x_sent(j, k)
        for k in range(7):
            z_sent(j, k)
        c_sent(j)
        for k in range(4):
            g_y(j, k, True).wait_send()
        return carry

    lax.fori_loop(0, NCH, in_done, 0)
    for k in range(3):
        n_copy(k, False).wait_recv()
    cnt[...] = (cntbuf[0] + cntbuf[1] + cntbuf[2] + cntbuf[3]) * (1.0 / MOST)
    loads[2].wait()

    def o_y(j, k, sent):
        to = (y_up, y_dn)[k % 2]
        if k < 2:
            src = xs.at[j, y_op, pl.ds(k * half, half)]
            dst = ryh.at[j, k]
        else:
            src = xs.at[j, to]
            dst = ryf.at[j, k - 2]
        return remote(src, dst, yo_s.at[j, k], yo_r.at[j, k], at_y(to))

    def o_c(j):
        return remote(cblock(dense.at[j], 1 - c), crecv.at[j], co_s.at[j], co_r.at[j], other)

    z_steps = ((4, 1), (3, 1), (2, 1), (1, 1), (-3, -1), (-2, -1), (-1, -1))

    def o_z(j, k):
        off, hop = z_steps[k]
        return remote(zblock(dense.at[j], c, zat(off)), zrecv.at[j, k],
                      zo_s.at[j, k], zo_r.at[j, k], at_z(hop))

    x_steps = ((2, 1), (1, 1), (-1, -1))

    def o_x(j, k):
        off, hop = x_steps[k]
        return remote(xblock(dense.at[j], c, z, xat(off)), xrecv.at[j, pl.ds(k, 1)],
                      xo_s.at[j, k], xo_r.at[j, k], at_x(hop))

    def add(a, b):
        return (a.astype(F32) + b.astype(F32)).astype(BF16)

    def add_z(j, k):
        off, hop = z_steps[k]
        o_z(j, k).wait_recv()
        at = pl.ds(c * NZ * NX + zat(off - hop) * NX, NX)
        dense[j, at] = add(dense[j, at], zrecv[j, k])

    def o0(j):
        cols = pl.ds(pl.multiple_of(j * CW, CW), CW)
        for e in range(EXP_DEV):
            parts = []
            for r in range(FF // BLOCK):
                row = jnp.concatenate(
                    [jnp.full((1, BLOCK), ds[e, r * (D // BLOCK) + j * RB + i], F32) for i in range(RB)],
                    axis=1,
                )
                rows = dq[e, r * BLOCK:(r + 1) * BLOCK, cols]
                parts.append((rows.astype(F32) * row).astype(BF16))
            w = jnp.concatenate(parts, axis=0)
            out = jnp.dot(hid[e], w, preferred_element_type=F32).astype(BF16)
            xs[j, :, e * CAP:(e + 1) * CAP, :] = out.reshape(NY, CAP, CW)
        o_y(j, 0, True).start()
        o_y(j, 1, True).start()

    def o1(j):
        for k in range(2):
            o_y(j, k, False).wait_recv()
            to = (y_up, y_dn)[k]
            at = pl.ds(k * half, half)
            xs[j, to, at] = add(xs[j, to, at], ryh[j, k])
            o_y(j, 2 + k, True).start()

    def o2(j):
        o_y(j, 2, False).wait_recv()
        o_y(j, 3, False).wait_recv()
        total = xs[j, y].astype(F32) + ryf[j, 0].astype(F32) + ryf[j, 1].astype(F32)
        scaled = (total * wslot[:, 0:1]).astype(BF16)
        n = 256
        for i in range(PLANE // n):
            out = jnp.dot(unpack[i * n:(i + 1) * n, :], scaled, preferred_element_type=F32)
            dense[j, i * (n // ROWS):(i + 1) * (n // ROWS)] = out.astype(BF16).reshape(n // ROWS, ROWS, CW)
        o_c(j).start()

    def o3(j):
        o_c(j).wait_recv()
        at = pl.ds(c * NZ * NX, NZ * NX)
        dense[j, at] = add(dense[j, at], crecv[j])
        o_z(j, 0).start()
        o_z(j, 4).start()

    def o4(j):
        add_z(j, 0)
        o_z(j, 1).start()
        add_z(j, 4)
        o_z(j, 5).start()

    def o5(j):
        add_z(j, 1)
        o_z(j, 2).start()
        add_z(j, 5)
        o_z(j, 6).start()

    def o6(j):
        add_z(j, 2)
        o_z(j, 3).start()

    def o7(j):
        add_z(j, 3)
        add_z(j, 6)
        o_x(j, 0).start()
        o_x(j, 2).start()

    def o8(j):
        o_x(j, 0).wait_recv()
        at = c * NZ * NX + z * NX + xat(1)
        dense[j, at] = add(dense[j, at], xrecv[j, 0])
        o_x(j, 1).start()

    def o9(j):
        o_x(j, 1).wait_recv()
        o_x(j, 2).wait_recv()
        total = dense[j, own].astype(F32) + xrecv[j, 1].astype(F32) + xrecv[j, 2].astype(F32)
        comb[:, pl.ds(pl.multiple_of(j * CW, CW), CW)] = total.astype(BF16)

    def out_tick(t, carry):
        for late, fn in enumerate((o0, o1, o2, o3, o4, o5, o6, o7, o8, o9)):
            stage(t, late, fn)
        return carry

    lax.fori_loop(0, NCH + 9, out_tick, 0)

    def out_done(j, carry):
        for k in range(4):
            o_y(j, k, True).wait_send()
        o_c(j).wait_send()
        for k in range(7):
            o_z(j, k).wait_send()
        for k in range(3):
            o_x(j, k).wait_send()
        return carry

    lax.fori_loop(0, NCH, out_done, 0)
    for k in range(3):
        n_copy(k, True).wait_send()


def layer(tok, meta, gs, us, ds, gq, uq, dq):
    vmem = pl.BlockSpec(memory_space=pltpu.VMEM)
    smem = pl.BlockSpec(memory_space=pltpu.SMEM)
    hbm = pl.BlockSpec(memory_space=pl.ANY)
    dma = pltpu.SemaphoreType.DMA
    blocks = NC * NZ * NX
    return pl.pallas_call(
        kernel,
        out_shape=(
            jax.ShapeDtypeStruct((ROWS, D), BF16),
            jax.ShapeDtypeStruct((8, N_EP * NY), F32),
        ),
        in_specs=[vmem, vmem, smem, smem, smem, hbm, hbm, hbm],
        out_specs=(vmem, vmem),
        scratch_shapes=[
            pltpu.VMEM((NCH, blocks, ROWS, CW), BF16),
            pltpu.VMEM((blocks, ROWS, BLOCK), BF16),
            pltpu.VMEM((NCH, NY, SLOTS, CW), BF16),
            pltpu.VMEM((EXP_DEV, D, FF), BF16),
            pltpu.VMEM((EXP_DEV, D, FF), BF16),
            pltpu.VMEM((EXP_DEV, FF, D), BF16),
            pltpu.VMEM((EXP_DEV, NY * CAP, FF), F32),
            pltpu.VMEM((EXP_DEV, NY * CAP, FF), F32),
            pltpu.VMEM((EXP_DEV, NY * CAP, FF), BF16),
            pltpu.VMEM((NCH, 2, SLOTS // 2, CW), BF16),
            pltpu.VMEM((NCH, 2, SLOTS, CW), BF16),
            pltpu.VMEM((NCH, blocks // 2, ROWS, CW), BF16),
            pltpu.VMEM((NCH, 7, NX, ROWS, CW), BF16),
            pltpu.VMEM((NCH, 3, ROWS, CW), BF16),
            pltpu.VMEM((SLOTS, PLANE), BF16),
            pltpu.VMEM((PLANE, SLOTS), BF16),
            pltpu.VMEM((SLOTS, BLOCK), F32),
            pltpu.VMEM((NY, 8, N_EP * NY), F32),
            dma((3,)),
            dma((NCH, 3)), dma((NCH, 3)),
            dma((NCH, 7)), dma((NCH, 7)),
            dma((NCH,)), dma((NCH,)),
            dma((NCH, 4)), dma((NCH, 4)),
            dma((11,)), dma((11,)),
            dma((NCH, 4)), dma((NCH, 4)),
            dma((NCH,)), dma((NCH,)),
            dma((NCH, 7)), dma((NCH, 7)),
            dma((NCH, 3)), dma((NCH, 3)),
            dma((3,)), dma((3,)),
        ],
        compiler_params=pltpu.CompilerParams(
            collective_id=0, has_side_effects=True, vmem_limit_bytes=60 * 1024 * 1024
        ),
        cost_estimate=pl.CostEstimate(
            flops=6_000_000_000, bytes_accessed=400_000_000, transcendentals=0
        ),
    )(tok, meta, gs, us, ds, gq, uq, dq)


def slot_keys(top_ids, replica_pick, plan):
    home = top_ids // EXP_DEV
    partner = (home + N_EP // 2) % N_EP
    held = jnp.sum(
        jnp.where(partner[..., None] == jnp.arange(N_EP, dtype=jnp.int32), plan, 0), axis=-1
    )
    moved = (held == top_ids) & (replica_pick == 1)
    target = jnp.where(moved, partner, home)
    return target * (EXP_DEV + 1) + jnp.where(moved, EXP_DEV, top_ids % EXP_DEV)


def per_device(
    tokens, top_ids, gate_int, replica_pick, plan,
    gate_q, gate_scale, up_q, up_scale, down_q, down_scale,
):
    ep = lax.axis_index("ep")
    receiver = (ep + N_EP // 2) % N_EP
    wanted = plan[receiver] - ep * EXP_DEV
    route = [((i + N_EP // 2) % N_EP, i) for i in range(N_EP)]
    moved_down, moved_scale = (
        lax.ppermute(lax.dynamic_index_in_dim(a, wanted, 0, keepdims=True), "ep", route)
        for a in (down_q, down_scale)
    )
    keys = slot_keys(top_ids, replica_pick, plan)
    meta = jnp.concatenate([top_ids, gate_int, keys], axis=1).astype(BF16)
    meta = jnp.pad(meta, ((0, 0), (0, BLOCK - 3 * TOPK)))
    combined, fill = layer(
        tokens, meta,
        gate_scale.astype(F32).reshape(EXP_DEV, -1),
        up_scale.astype(F32).reshape(EXP_DEV, -1),
        down_scale.astype(F32).reshape(EXP_DEV, -1),
        gate_q, up_q, down_q,
    )
    return combined, fill[None, :EXP_DEV + 1], moved_down, moved_scale


def solution(mesh):
    return jax.shard_map(
        per_device,
        mesh=mesh,
        in_specs=(
            P(("ep", "dp"), None),
            P(("ep", "dp"), None),
            P(("ep", "dp"), None),
            P(("ep", "dp"), None),
            P(),
            P("ep", None, "dp"),
            P("ep", None, "dp"),
            P("ep", None, "dp"),
            P("ep", None, "dp"),
            P("ep", "dp", None),
            P("ep", "dp", None),
        ),
        out_specs=(
            P(("ep", "dp"), None),
            P("ep", None, None),
            P("ep", "dp", None),
            P("ep", "dp", None),
        ),
        check_vma=False,
    )
```

time: 493 us -> 248 us (0.50)
  waiting for transfers between devices: 241 us -> 0.01 us
  Pallas kernels: 0 us -> 230 us
  blocking collectives: 88.4 us -> 0 us
  local copies, waits for them, and re-layouts: 69 us -> 11.3 us
  starting transfers between devices: 28.5 us -> 3.53 us
  matrix products: 24.4 us -> 0 us
  other arithmetic: 22.9 us -> 1.14 us
  between operations: 15.2 us -> 1.4 us
    pallas_call x0 -> x1, Pallas kernels: none -> 230 us  [layer(): pl.pallas_call(kernel, out_shape=(jax.ShapeDtypeStruct((ROWS, D), BF16),...]
    ppermute x6 -> x2, waiting for transfers between devices: 95.6 us -> 0.01 us  [per_device(): lax.ppermute(lax.dynamic_index_in_dim(a, wanted, 0, keepdims=True), 'ep',...]
    reduce_scatter x1 -> x0, waiting for transfers between devices: 94.5 us -> none  [per_device(): lax.psum_scatter(apply_slots(gathered, slot_weights).astype(jnp.bfloat16)...]
    all_to_all x1 -> x0, blocking collectives: 76.4 us -> none  [per_device(): lax.all_to_all(outgoing, 'ep', split_axis=0, concat_axis=0, tiled=True)]
    all_to_all x2 -> x0, waiting for transfers between devices: 50.7 us -> none  [the longest x1 50.7 us: per_device(): lax.all_to_all(summed, 'ep', split_axis=0, concat_axis=0, tiled=True)]
    another operation x6 -> x2, local copies, waits for them, and re-layouts: 25.5 us -> 0.17 us  [the longest x3 25.2 us: apply_slots(): flat_rows = block[:, index].reshape(-1, block.shape[-1])]
    dot_general x11 -> x0, matrix products: 24.4 us -> none  [the longest x3 11.6 us: apply_slots(): gate_v = jnp.dot(flat_rows, gate_w, preferred_element_type=jnp.float32)]
    all_to_all x2 -> x0, starting transfers between devices: 16.7 us -> none  [the longest x1 10.6 us: per_device(): lax.all_to_all(summed, 'ep', split_axis=0, concat_axis=0, tiled=True)]
  transfers between devices with their start and end apart: 10 -> 2, of which waited for: 5 -> 0; matrix products, arithmetic and copies ran while one was open for 7% -> 2% of each run, Pallas kernels for 0% -> 93%
where the time goes in v1:
time: 248 us
  Pallas kernels  230 us (93%)
  local copies, waits for them, and re-layouts  11.3 us (5%)
  starting transfers between devices  3.53 us (1%)
    pallas_call x1, Pallas kernels, layer(): pl.pallas_call(kernel, out_shape=(jax.ShapeDtypeStruct((ROWS, D), BF16),...  230 us
  transfers between devices with their start and end apart: 2, of which 0 were waited for; matrix products, arithmetic and copies ran while one was open for 2% of the time, Pallas kernels for 93%

profile of v1, /device:TPU:2, one launch (start us, length us, event | category | flops | bytes accessed | tf_op | source)
XLA Modules:
  0.0 247.6 jit_solution(18221006742681045370)
XLA Ops:
  0.6 0.0 copy-start.6
  0.6 0.0 copy-start.5
  0.7 0.0 copy-start
  0.7 0.0 copy-start.1
  0.7 0.0 copy-start.2
  0.7 1.3 dynamic_slice.11
  2.6 2.9 %constant_dynamic-slice_fusion = bf16[1,256,3584]{2,1,0:T(8,128)(2,1)} fusion(bf16[2,256,3584]{2,1,0:T(8,128)(2,1)} %dq_hbm.1, s32[]{:T(128)S(6)} %select_n.50), kind=kLoop, calls=%fused_computation.24 | loop fusion | bytes 3670020 | tf_op jit(solution)/shard_map/jit(dynamic_index_in_dim)/dynamic_slice | solution.py:553
  5.5 2.1 collective-permute-start
  7.6 0.0 copy-done.5
  7.6 1.4 collective-permute-start.1
  9.0 0.1 copy.48
  9.1 0.7 reshape.35.ds
  9.8 0.0 copy-done.1
  9.8 0.1 copy.53
  9.8 0.1 copy.54
  9.9 0.1 copy.55
  10.0 0.0 copy-done.3
  10.0 0.1 copy.56
  10.1 0.7 reshape.31.gs
  10.8 0.0 copy-done.4
  10.8 0.1 copy.57
  10.9 0.7 reshape.33.us
  11.6 0.4 select_reduce_fusion
  12.1 0.7 fusion.10.meta
  12.8 230.3 %shard_map.138 = (bf16[16,3584]{1,0:T(8,128)(2,1)}, f32[8,256]{1,0:T(8,128)}) custom-call(bf16[16,3584]{1,0:T(8,128)(2,1)} %tok.1, bf16[16,128]{1,0:T(8,128)(2,1)} %fusion.10.meta, f32[2,56]{1,0:T(2,128)} %reshape.31.gs, f32[2,56]{1,0:T(2,128)} %reshape.33.us, f32[2,56]{1,0:T(2,128)} %reshape.35.ds, bf16[2,3584,256]{2,1,0:T(8,128)(2,1)} %gq_hbm.1, ...), custom_call_target="tpu_custom_call" | custom-call | flops 6000000000 | bytes 400000000 | tf_op jit(solution)/shard_map/pallas_call | solution.py:485
  243.1 0.7 slice_bitcast_fusion
  243.8 0.6 copy.58
  244.3 0.0 collective-permute-done.1
  244.3 0.0 collective-permute-done
  244.3 1.6 copy.62
  245.9 1.2 copy.63
  247.1 0.5 copy.64
  (10 shorter events, 0.1 us)
Async XLA Ops:
  0.6 11.0 %copy-start.6 = (s32[64]{0:T(128)S(1)}, s32[64]{0:T(128)}, u32[]{:S(2)}) copy-start(s32[64]{0:T(128)} %param.15) | copy-start | bytes 772
  0.6 7.0 %copy-start.5 = (bf16[2,2,28]{2,1,0:T(2,128)(2,1)S(1)}, bf16[2,2,28]{2,1,0:T(2,128)(2,1)}, u32[]{:S(2)}) copy-start(bf16[2,2,28]{2,1,0:T(2,128)(2,1)} %param.21) | copy-start | bytes 676
  0.7 8.4 %copy-start = (s32[16,8]{0,1:T(8,128)S(1)}, s32[16,8]{0,1:T(8,128)}, u32[]{:S(2)}) copy-start(s32[16,8]{0,1:T(8,128)} %param.12) | copy-start | bytes 1540
  0.7 9.1 %copy-start.1 = (s32[16,8]{0,1:T(8,128)S(1)}, s32[16,8]{0,1:T(8,128)}, u32[]{:S(2)}) copy-start(s32[16,8]{0,1:T(8,128)} %param.14) | copy-start | bytes 1540
  0.7 9.2 %copy-start.2 = (s32[16,8]{0,1:T(8,128)S(1)}, s32[16,8]{0,1:T(8,128)}, u32[]{:S(2)}) copy-start(s32[16,8]{0,1:T(8,128)} %param.13) | copy-start | bytes 1540
  0.7 9.3 %copy-start.3 = (bf16[2,28,2]{1,2,0:T(2,128)(2,1)S(1)}, bf16[2,28,2]{1,2,0:T(2,128)(2,1)}, u32[]{:S(2)}) copy-start(bf16[2,28,2]{1,2,0:T(2,128)(2,1)} %param.17) | copy-start | bytes 676
  0.7 10.1 %copy-start.4 = (bf16[2,28,2]{1,2,0:T(2,128)(2,1)S(1)}, bf16[2,28,2]{1,2,0:T(2,128)(2,1)}, u32[]{:S(2)}) copy-start(bf16[2,28,2]{1,2,0:T(2,128)(2,1)} %param.19) | copy-start | bytes 676
  5.5 238.9 %collective-permute-start = (bf16[1,256,3584]{2,1,0:T(8,128)(2,1)}, bf16[1,256,3584]{2,1,0:T(8,128)(2,1)S(1)}, u32[]{:S(2)}, u32[]{:S(2)}) collective-permute-start(bf16[1,256,3584]{2,1,0:T(8,128)(2,1)} %constant_dynamic-slice_fusion), channel_id=1, source_target_pairs={{128,0},{132,4},{136,8},{140,12},{144,16},{148,20},{152,24},{156,2... | collective-permute-start | bytes 5505032 | tf_op jit(solution)/shard_map/ppermute | solution.py:553
  7.6 236.7 %collective-permute-start.1 = (bf16[1,2,28]{2,1,0:T(2,128)(2,1)S(1)}, bf16[1,2,28]{2,1,0:T(2,128)(2,1)S(1)}, u32[]{:S(2)}, u32[]{:S(2)}) collective-permute-start(bf16[1,2,28]{2,1,0:T(2,128)(2,1)S(1)} %constant_dynamic-slice_fusion.1), channel_id=1, source_target_pairs={{128,0},{132,4},{136,8},{140,12},{144,16},{148,20},{152,24},{156,2... | collective-permute-start | bytes 344 | tf_op jit(solution)/shard_map/ppermute | solution.py:553

commit v2 on v1

--- a/solution.py
+++ b/solution.py
@@ -19,7 +19,7 @@
 D = 3584
 FF = 256
 BLOCK = 128
-CW = 512
+CW = 256
 NCH = D // CW
 RB = CW // BLOCK
 F32 = jnp.float32
@@ -28,11 +28,11 @@
 
 
 def kernel(
-    tok, meta, gs, us, ds, gq_hbm, uq_hbm, dq_hbm,
-    comb, cnt,
+    tok, ids_t, gates_t, picks_t, plan, gs, us, ds, gq_hbm, uq_hbm, dq_hbm,
+    comb, cnt, moved, moved_s,
     dense, mg, xs, gq, uq, dq, accg, accu, hid, ryh, ryf, crecv, zrecv, xrecv,
-    pack, unpack, wslot, cntbuf,
-    w_sem, xi_s, xi_r, zi_s, zi_r, ci_s, ci_r, yi_s, yi_r, m_s, m_r,
+    pack, unpack, wslot, cntbuf, sel, sel_s, got_s, grow, urow, drow,
+    w_sem, mv_s, mv_r, xi_s, xi_r, zi_s, zi_r, ci_s, ci_r, yi_s, yi_r, m_s, m_r,
     yo_s, yo_r, co_s, co_r, zo_s, zo_r, xo_s, xo_r, n_s, n_r,
 ):
     ep = lax.axis_index("ep")
@@ -76,35 +76,29 @@
         return ref.at[pl.ds(core * NZ * NX, NZ * NX)]
 
     def g_x(ref, ss, rs, k, sent):
-        off, hop = ((0, 1), (-1, 1), (0, -1))[k]
-        if not sent:
-            off = off - hop
-        b = xblock(ref, c, z, xat(off))
+        hop = (1, -1, 2)[k]
+        b = xblock(ref, c, z, xat(0 if sent else -hop))
         return remote(b, b, ss, rs, at_x(hop))
 
     def g_z(ref, ss, rs, k, sent):
-        off, hop = ((0, 1), (-1, 1), (-2, 1), (-3, 1), (0, -1), (1, -1), (2, -1))[k]
+        off, hop = ((0, 1), (0, -1), (0, 2), (0, -2), (-2, 1), (2, -1), (-2, 2))[k]
         if not sent:
             off = off - hop
         b = zblock(ref, c, zat(off))
         return remote(b, b, ss, rs, at_z(hop))
 
-    def g_c(ref, ss, rs, off):
-        b = zblock(ref, c, zat(off))
-        return remote(b, b, ss, rs, other)
-
-    def g_c_all(ref, ss, rs, core):
+    def g_c(ref, ss, rs, core):
         b = cblock(ref, core)
         return remote(b, b, ss, rs, other)
 
     def both(j, fn):
-        fn(dense.at[j], (xi_s.at[j], xi_r.at[j], zi_s.at[j], zi_r.at[j], ci_s.at[j], ci_r.at[j]))
-
         @pl.when(j == 0)
         def _():
             fn(mg, (m_s.at[pl.ds(0, 3)], m_r.at[pl.ds(0, 3)], m_s.at[pl.ds(3, 7)],
                     m_r.at[pl.ds(3, 7)], m_s.at[10], m_r.at[10]))
 
+        fn(dense.at[j], (xi_s.at[j], xi_r.at[j], zi_s.at[j], zi_r.at[j], ci_s.at[j], ci_r.at[j]))
+
     def x_start(j, k):
         both(j, lambda ref, q: g_x(ref, q[0].at[k], q[1].at[k], k, True).start())
 
@@ -123,14 +117,14 @@
     def z_sent(j, k):
         both(j, lambda ref, q: g_z(ref, q[2].at[k], q[3].at[k], k, True).wait_send())
 
-    def c_start(j, off):
-        both(j, lambda ref, q: g_c(ref, q[4], q[5], off).start())
+    def c_start(j):
+        both(j, lambda ref, q: g_c(ref, q[4], q[5], c).start())
 
     def c_recv(j):
-        both(j, lambda ref, q: g_c_all(ref, q[4], q[5], 1 - c).wait_recv())
+        both(j, lambda ref, q: g_c(ref, q[4], q[5], 1 - c).wait_recv())
 
     def c_sent(j):
-        both(j, lambda ref, q: g_c_all(ref, q[4], q[5], c).wait_send())
+        both(j, lambda ref, q: g_c(ref, q[4], q[5], c).wait_send())
 
     half = SLOTS // 2
 
@@ -144,8 +138,55 @@
             b = xs.at[j, plane, pl.ds((k - 2) * half, half)]
         return remote(b, b, yi_s.at[j, k], yi_r.at[j, k], at_y(to))
 
+    def routing_values():
+        ids = ids_t[...]
+        planned = ids == plan[0]
+        for r in range(1, N_EP):
+            planned = planned | (ids == plan[r])
+        there = planned & (picks_t[...] == 1)
+        home = ids >> 1
+        target = jnp.where(there, (home + N_EP // 2) & (N_EP - 1), home)
+        key = target * (EXP_DEV + 1) + jnp.where(there, EXP_DEV, ids & 1)
+        cols = jnp.concatenate([ids, gates_t[...], key], axis=0).astype(F32).astype(BF16)
+        n = 3 * TOPK
+        place = lax.broadcasted_iota(jnp.int32, (n, BLOCK), 0) == lax.broadcasted_iota(jnp.int32, (n, BLOCK), 1)
+        return lax.dot_general(
+            cols, place.astype(BF16), (((0,), (0,)), ((), ())), preferred_element_type=F32
+        ).astype(BF16)
+
+    def spread_scales():
+        side = lax.broadcasted_iota(jnp.int32, (2, FF), 0) == lax.broadcasted_iota(jnp.int32, (2, FF), 1) // BLOCK
+        n = D // BLOCK
+        wide = lax.broadcasted_iota(jnp.int32, (n, D), 0) == lax.broadcasted_iota(jnp.int32, (n, D), 1) // BLOCK
+        for e in range(EXP_DEV):
+            for src, dst in ((gs, grow), (us, urow)):
+                dst[e] = lax.dot_general(
+                    src[e], side.astype(BF16), (((0,), (0,)), ((), ())), preferred_element_type=F32
+                )
+            drow[e] = jnp.dot(ds[e], wide.astype(BF16), preferred_element_type=F32)
+
+    def mv(j):
+        cols = slice(None) if j is None else pl.ds(pl.multiple_of(j * CW, CW), CW)
+        return remote(sel.at[:, cols], moved.at[0, :, cols], mv_s.at[0], mv_r.at[0], at_x(2))
+
+    def mv_scale():
+        return remote(sel_s, got_s, mv_s.at[1], mv_r.at[1], at_x(2))
+
+    def select_moved():
+        loads[2].wait()
+        wanted = plan[(ep + N_EP // 2) % N_EP] - ep * EXP_DEV
+        for i in range(FF // BLOCK):
+            at = slice(i * BLOCK, (i + 1) * BLOCK)
+            sel[at, :] = jnp.where(wanted == 0, dq[0, at, :], dq[1, at, :])
+        sel_s[...] = jnp.zeros_like(sel_s)
+        sel_s[0:FF // BLOCK, 0:D // BLOCK] = jnp.where(wanted == 0, ds[0], ds[1])
+        mv_scale().start()
+
     barrier = pltpu.get_barrier_semaphore()
-    partners = (at_x(1), at_x(-1), at_z(1), at_z(-1), other, at_y(y_up), at_y(y_dn), at_y(y_op))
+    partners = (
+        at_x(1), at_x(-1), at_x(2), at_z(1), at_z(-1), at_z(2), at_z(-2), other,
+        at_y(y_up), at_y(y_dn), at_y(y_op),
+    )
     for dev in partners:
         pl.semaphore_signal(barrier, inc=1, device_id=dev, device_id_type=MESH)
 
@@ -156,7 +197,8 @@
     for load in loads:
         load.start()
     own = c * NZ * NX + z * NX + x
-    mg[own] = meta[...]
+    mg[own] = routing_values()
+    spread_scales()
     for j in range(NCH):
         dense[j, own] = tok[:, j * CW:(j + 1) * CW]
     accg[...] = jnp.zeros_like(accg)
@@ -164,8 +206,8 @@
     pl.semaphore_wait(barrier, len(partners))
 
     def x_begin(j, carry):
-        x_start(j, 0)
-        x_start(j, 2)
+        for k in range(3):
+            x_start(j, k)
         return carry
 
     lax.fori_loop(0, NCH, x_begin, 0)
@@ -175,16 +217,35 @@
         b = cntbuf.at[y if sent else (y_dn, y_up, y_op)[k]]
         return remote(b, b, n_s.at[k], n_r.at[k], at_y(to))
 
+    def rows_of(i):
+        return mg[pl.ds(i * 8, 8)].reshape(BLOCK, BLOCK).astype(F32)
+
+    def fill_slots():
+        lane = lax.broadcasted_iota(jnp.int32, (BLOCK, BLOCK), 1)
+        slot0 = (ep * (EXP_DEV + 1)).astype(F32)
+        fills = jnp.zeros((BLOCK, N_EP * NY), F32)
+        for i in range(PLANE // BLOCK):
+            m = rows_of(i)
+            keyed = (lane >= 2 * TOPK) & (lane < 3 * TOPK)
+            tally = jnp.zeros((BLOCK, BLOCK), F32)
+            for s in range(EXP_DEV + 1):
+                n = jnp.sum(jnp.where(keyed & (m == slot0 + s), 1.0, 0.0), axis=1, keepdims=True)
+                tally = tally + jnp.where(lane == s, n, 0.0)
+            r = lax.broadcasted_iota(jnp.int32, (BLOCK, N_EP * NY), 0) + i * BLOCK
+            col = lax.broadcasted_iota(jnp.int32, (BLOCK, N_EP * NY), 1)
+            b = r >> 4
+            source = (b & 3) * (NZ * NC) + ((b >> 2) & 7) * NC + (b >> 5)
+            mine = (col == source * NY + y).astype(BF16)
+            fills = fills + jnp.dot(jnp.transpose(tally).astype(BF16), mine, preferred_element_type=F32)
+        cntbuf[y] = fills[0:8]
+        for k in range(3):
+            n_copy(k, True).start()
+
     def routes():
-        def rows_of(i):
-            return mg[pl.ds(i * 8, 8)].reshape(BLOCK, BLOCK).astype(F32)
-
         lane = lax.broadcasted_iota(jnp.int32, (BLOCK, BLOCK), 1)
         row = lax.broadcasted_iota(jnp.int32, (BLOCK, BLOCK), 0)
         before = (lane < row).astype(BF16)
         first = (ep * EXP_DEV).astype(F32)
-        slot0 = (ep * (EXP_DEV + 1)).astype(F32)
-        fills = jnp.zeros((BLOCK, N_EP * NY), F32)
         sofar = jnp.zeros((1, BLOCK), F32)
         wsum = jnp.zeros((SLOTS, 1), F32)
         for i in range(PLANE // BLOCK):
@@ -211,29 +272,12 @@
             turned = jnp.transpose(spread)
             pack[:, i * BLOCK:(i + 1) * BLOCK] = jnp.where(turned > 0.0, 1.0, 0.0).astype(BF16)
             wsum = wsum + jnp.sum(turned, axis=1, keepdims=True)
-            keyed = (lane >= 2 * TOPK) & (lane < 3 * TOPK)
-            tally = jnp.zeros((BLOCK, BLOCK), F32)
-            for s in range(EXP_DEV + 1):
-                n = jnp.sum(jnp.where(keyed & (m == slot0 + s), 1.0, 0.0), axis=1, keepdims=True)
-                tally = tally + jnp.where(lane == s, n, 0.0)
-            r = lax.broadcasted_iota(jnp.int32, (BLOCK, N_EP * NY), 0) + i * BLOCK
-            col = lax.broadcasted_iota(jnp.int32, (BLOCK, N_EP * NY), 1)
-            b = r >> 4
-            source = (b & 3) * (NZ * NC) + ((b >> 2) & 7) * NC + (b >> 5)
-            mine = (col == source * NY + y).astype(BF16)
-            fills = fills + jnp.dot(jnp.transpose(tally).astype(BF16), mine, preferred_element_type=F32)
         wslot[...] = jnp.broadcast_to(wsum, (SLOTS, BLOCK))
-        cntbuf[y] = fills[0:8]
-        for k in range(3):
-            n_copy(k, True).start()
 
     def weight(q, e, j, s):
         parts = []
         for i in range(RB):
-            at = (j * RB + i) * 2
-            row = jnp.where(
-                lax.broadcasted_iota(jnp.int32, (1, FF), 1) < BLOCK, s[e, at], s[e, at + 1]
-            )
+            row = s[e, pl.ds(j * RB + i, 1), :]
             rows = q[e, pl.ds(pl.multiple_of(j * CW + i * BLOCK, BLOCK), BLOCK), :]
             parts.append((rows.astype(F32) * row).astype(BF16))
         return jnp.concatenate(parts, axis=0)
@@ -246,42 +290,22 @@
             fn(j)
 
     def i1(j):
-        x_recv(j, 0)
-        x_start(j, 1)
+        for k in range(3):
+            x_recv(j, k)
+        for k in range(4):
+            z_start(j, k)
 
     def i2(j):
-        x_recv(j, 2)
-        x_recv(j, 1)
-        z_start(j, 0)
+        z_recv(j, 2)
         z_start(j, 4)
-        c_start(j, 0)
+        z_start(j, 6)
+        z_recv(j, 3)
+        z_start(j, 5)
 
     def i3(j):
-        z_recv(j, 0)
-        z_start(j, 1)
-        z_recv(j, 4)
-        z_start(j, 5)
-        c_start(j, -1)
-        c_start(j, 1)
-
-    def i4(j):
-        z_recv(j, 1)
-        z_start(j, 2)
-        z_recv(j, 5)
-        z_start(j, 6)
-        c_start(j, -2)
-        c_start(j, 2)
-
-    def i5(j):
-        z_recv(j, 2)
-        z_start(j, 3)
-        c_start(j, -3)
-        z_recv(j, 6)
-        c_start(j, 3)
-
-    def i6(j):
-        z_recv(j, 3)
-        c_start(j, -4)
+        for k in (0, 1, 4, 5, 6):
+            z_recv(j, k)
+        c_start(j)
 
     def i7(j):
         c_recv(j)
@@ -311,15 +335,29 @@
         g_y(j, 3, False).wait_recv()
         for e in range(EXP_DEV):
             rows = xs[j, :, e * CAP:(e + 1) * CAP, :].reshape(NY * CAP, CW)
-            accg[e] += jnp.dot(rows, weight(gq, e, j, gs), preferred_element_type=F32)
-            accu[e] += jnp.dot(rows, weight(uq, e, j, us), preferred_element_type=F32)
+            accg[e] += jnp.dot(rows, weight(gq, e, j, grow), preferred_element_type=F32)
+            accu[e] += jnp.dot(rows, weight(uq, e, j, urow), preferred_element_type=F32)
 
     def in_tick(t, carry):
-        for late, fn in enumerate((i1, i2, i3, i4, i5, i6, i7, i8, i9)):
-            stage(t, late, fn)
+        stage(t, 5, i7)
+        stage(t, 4, i3)
+        stage(t, 2, i2)
+        stage(t, 0, i1)
+
+        @pl.when(t == 6)
+        def _():
+            select_moved()
+
+        @pl.when(t == 8)
+        def _():
+            fill_slots()
+
+        stage(t, 6, lambda j: mv(j).start())
+        stage(t, 7, i8)
+        stage(t, 9, i9)
         return carry
 
-    lax.fori_loop(0, NCH + 8, in_tick, 0)
+    lax.fori_loop(0, NCH + 9, in_tick, 0)
 
     for e in range(EXP_DEV):
         v = accg[e]
@@ -338,8 +376,8 @@
     lax.fori_loop(0, NCH, in_done, 0)
     for k in range(3):
         n_copy(k, False).wait_recv()
-    cnt[...] = (cntbuf[0] + cntbuf[1] + cntbuf[2] + cntbuf[3]) * (1.0 / MOST)
-    loads[2].wait()
+    total = (cntbuf[0] + cntbuf[1] + cntbuf[2] + cntbuf[3]) * (1.0 / MOST)
+    cnt[0] = total[0:EXP_DEV + 1]
 
     def o_y(j, k, sent):
         to = (y_up, y_dn)[k % 2]
@@ -354,18 +392,16 @@
     def o_c(j):
         return remote(cblock(dense.at[j], 1 - c), crecv.at[j], co_s.at[j], co_r.at[j], other)
 
-    z_steps = ((4, 1), (3, 1), (2, 1), (1, 1), (-3, -1), (-2, -1), (-1, -1))
+    z_steps = ((3, 1), (-3, -1), (4, 2), (2, 2), (-2, -2), (1, 1), (-1, -1))
 
     def o_z(j, k):
         off, hop = z_steps[k]
         return remote(zblock(dense.at[j], c, zat(off)), zrecv.at[j, k],
                       zo_s.at[j, k], zo_r.at[j, k], at_z(hop))
 
-    x_steps = ((2, 1), (1, 1), (-1, -1))
-
     def o_x(j, k):
-        off, hop = x_steps[k]
-        return remote(xblock(dense.at[j], c, z, xat(off)), xrecv.at[j, pl.ds(k, 1)],
+        hop = (1, -1, 2)[k]
+        return remote(xblock(dense.at[j], c, z, xat(hop)), xrecv.at[j, pl.ds(k, 1)],
                       xo_s.at[j, k], xo_r.at[j, k], at_x(hop))
 
     def add(a, b):
@@ -382,10 +418,7 @@
         for e in range(EXP_DEV):
             parts = []
             for r in range(FF // BLOCK):
-                row = jnp.concatenate(
-                    [jnp.full((1, BLOCK), ds[e, r * (D // BLOCK) + j * RB + i], F32) for i in range(RB)],
-                    axis=1,
-                )
+                row = drow[e, r:r + 1, cols]
                 rows = dq[e, r * BLOCK:(r + 1) * BLOCK, cols]
                 parts.append((rows.astype(F32) * row).astype(BF16))
             w = jnp.concatenate(parts, axis=0)
@@ -417,49 +450,44 @@
         o_c(j).wait_recv()
         at = pl.ds(c * NZ * NX, NZ * NX)
         dense[j, at] = add(dense[j, at], crecv[j])
-        o_z(j, 0).start()
+        for k in (2, 0, 1, 5, 6):
+            o_z(j, k).start()
+
+    def o4(j):
+        for k in range(3):
+            add_z(j, k)
+        o_z(j, 3).start()
         o_z(j, 4).start()
 
-    def o4(j):
-        add_z(j, 0)
-        o_z(j, 1).start()
-        add_z(j, 4)
-        o_z(j, 5).start()
-
     def o5(j):
-        add_z(j, 1)
-        o_z(j, 2).start()
-        add_z(j, 5)
-        o_z(j, 6).start()
+        for k in range(3, 7):
+            o_z(j, k).wait_recv()
+        at = pl.ds(c * NZ * NX + z * NX, NX)
+        total = dense[j, at].astype(F32)
+        for k in range(3, 7):
+            total = total + zrecv[j, k].astype(F32)
+        dense[j, at] = total.astype(BF16)
+        for k in range(3):
+            o_x(j, k).start()
 
     def o6(j):
-        add_z(j, 2)
-        o_z(j, 3).start()
-
-    def o7(j):
-        add_z(j, 3)
-        add_z(j, 6)
-        o_x(j, 0).start()
-        o_x(j, 2).start()
-
-    def o8(j):
-        o_x(j, 0).wait_recv()
-        at = c * NZ * NX + z * NX + xat(1)
-        dense[j, at] = add(dense[j, at], xrecv[j, 0])
-        o_x(j, 1).start()
-
-    def o9(j):
-        o_x(j, 1).wait_recv()
-        o_x(j, 2).wait_recv()
-        total = dense[j, own].astype(F32) + xrecv[j, 1].astype(F32) + xrecv[j, 2].astype(F32)
+        total = dense[j, own].astype(F32)
+        for k in range(3):
+            o_x(j, k).wait_recv()
+            total = total + xrecv[j, k].astype(F32)
         comb[:, pl.ds(pl.multiple_of(j * CW, CW), CW)] = total.astype(BF16)
 
     def out_tick(t, carry):
-        for late, fn in enumerate((o0, o1, o2, o3, o4, o5, o6, o7, o8, o9)):
-            stage(t, late, fn)
+        stage(t, 0, o0)
+        stage(t, 2, o1)
+        stage(t, 5, o3)
+        stage(t, 7, o4)
+        stage(t, 9, o5)
+        stage(t, 11, o6)
+        stage(t, 4, o2)
         return carry
 
-    lax.fori_loop(0, NCH + 9, out_tick, 0)
+    lax.fori_loop(0, NCH + 11, out_tick, 0)
 
     def out_done(j, carry):
         for k in range(4):
@@ -474,9 +502,12 @@
     lax.fori_loop(0, NCH, out_done, 0)
     for k in range(3):
         n_copy(k, True).wait_send()
-
-
-def layer(tok, meta, gs, us, ds, gq, uq, dq):
+    mv(None).wait()
+    mv_scale().wait()
+    moved_s[0] = got_s[0:FF // BLOCK, 0:D // BLOCK]
+
+
+def layer(*args):
     vmem = pl.BlockSpec(memory_space=pltpu.VMEM)
     smem = pl.BlockSpec(memory_space=pltpu.SMEM)
     hbm = pl.BlockSpec(memory_space=pl.ANY)
@@ -486,10 +517,12 @@
         kernel,
         out_shape=(
             jax.ShapeDtypeStruct((ROWS, D), BF16),
-            jax.ShapeDtypeStruct((8, N_EP * NY), F32),
+            jax.ShapeDtypeStruct((1, EXP_DEV + 1, N_EP * NY), F32),
+            jax.ShapeDtypeStruct((1, FF, D), BF16),
+            jax.ShapeDtypeStruct((1, FF // BLOCK, D // BLOCK), BF16),
         ),
-        in_specs=[vmem, vmem, smem, smem, smem, hbm, hbm, hbm],
-        out_specs=(vmem, vmem),
+        in_specs=[vmem] * 4 + [smem] + [vmem] * 3 + [hbm] * 3,
+        out_specs=(vmem, vmem, hbm, vmem),
         scratch_shapes=[
             pltpu.VMEM((NCH, blocks, ROWS, CW), BF16),
             pltpu.VMEM((blocks, ROWS, BLOCK), BF16),
@@ -509,7 +542,14 @@
             pltpu.VMEM((PLANE, SLOTS), BF16),
             pltpu.VMEM((SLOTS, BLOCK), F32),
             pltpu.VMEM((NY, 8, N_EP * NY), F32),
+            pltpu.VMEM((FF, D), BF16),
+            pltpu.VMEM((ROWS, BLOCK), BF16),
+            pltpu.VMEM((ROWS, BLOCK), BF16),
+            pltpu.VMEM((EXP_DEV, D // BLOCK, FF), F32),
+            pltpu.VMEM((EXP_DEV, D // BLOCK, FF), F32),
+            pltpu.VMEM((EXP_DEV, FF // BLOCK, D), F32),
             dma((3,)),
+            dma((2,)), dma((2,)),
             dma((NCH, 3)), dma((NCH, 3)),
             dma((NCH, 7)), dma((NCH, 7)),
             dma((NCH,)), dma((NCH,)),
@@ -527,43 +567,18 @@
         cost_estimate=pl.CostEstimate(
             flops=6_000_000_000, bytes_accessed=400_000_000, transcendentals=0
         ),
-    )(tok, meta, gs, us, ds, gq, uq, dq)
-
-
-def slot_keys(top_ids, replica_pick, plan):
-    home = top_ids // EXP_DEV
-    partner = (home + N_EP // 2) % N_EP
-    held = jnp.sum(
-        jnp.where(partner[..., None] == jnp.arange(N_EP, dtype=jnp.int32), plan, 0), axis=-1
-    )
-    moved = (held == top_ids) & (replica_pick == 1)
-    target = jnp.where(moved, partner, home)
-    return target * (EXP_DEV + 1) + jnp.where(moved, EXP_DEV, top_ids % EXP_DEV)
+    )(*args)
 
 
 def per_device(
     tokens, top_ids, gate_int, replica_pick, plan,
     gate_q, gate_scale, up_q, up_scale, down_q, down_scale,
 ):
-    ep = lax.axis_index("ep")
-    receiver = (ep + N_EP // 2) % N_EP
-    wanted = plan[receiver] - ep * EXP_DEV
-    route = [((i + N_EP // 2) % N_EP, i) for i in range(N_EP)]
-    moved_down, moved_scale = (
-        lax.ppermute(lax.dynamic_index_in_dim(a, wanted, 0, keepdims=True), "ep", route)
-        for a in (down_q, down_scale)
-    )
-    keys = slot_keys(top_ids, replica_pick, plan)
-    meta = jnp.concatenate([top_ids, gate_int, keys], axis=1).astype(BF16)
-    meta = jnp.pad(meta, ((0, 0), (0, BLOCK - 3 * TOPK)))
-    combined, fill = layer(
-        tokens, meta,
-        gate_scale.astype(F32).reshape(EXP_DEV, -1),
-        up_scale.astype(F32).reshape(EXP_DEV, -1),
-        down_scale.astype(F32).reshape(EXP_DEV, -1),
+    return layer(
+        tokens, top_ids.T, gate_int.T, replica_pick.T, plan,
+        gate_scale.transpose(0, 2, 1), up_scale.transpose(0, 2, 1), down_scale,
         gate_q, up_q, down_q,
     )
-    return combined, fill[None, :EXP_DEV + 1], moved_down, moved_scale
 
 
 def solution(mesh):

time: 248 us -> 189 us (0.76)
  Pallas kernels: 230 us -> 181 us
  local copies, waits for them, and re-layouts: 11.3 us -> 6.17 us
  starting transfers between devices: 3.53 us -> 0 us
    pallas_call x1, Pallas kernels: 230 us -> 181 us  [layer(): pl.pallas_call(kernel, out_shape=(jax.ShapeDtypeStruct((ROWS, D), BF16),...]
    dynamic_slice x3 -> x0, local copies, waits for them, and re-layouts: 4.11 us -> none  [the longest x2 2.85 us: per_device(): lax.dynamic_index_in_dim(a, wanted, 0, keepdims=True)]
    ppermute x2 -> x0, starting transfers between devices: 3.53 us -> none  [per_device(): lax.ppermute(lax.dynamic_index_in_dim(a, wanted, 0, keepdims=True), 'ep',...]
  transfers between devices with their start and end apart: 2 -> 0, of which waited for: 0 -> 0; matrix products, arithmetic and copies ran while one was open for 2% -> 0% of each run, Pallas kernels for 93% -> 0%
where the time goes in v2:
time: 189 us; the launch traced here: 188 us
  Pallas kernels  181 us (96%)
  local copies, waits for them, and re-layouts  6.17 us (3%)
    pallas_call x1, Pallas kernels, layer(): pl.pallas_call(kernel, out_shape=(jax.ShapeDtypeStruct((ROWS, D), BF16),...  181 us
    unnamed x5, local copies, waits for them, and re-layouts  4.91 us

profile of v2, /device:TPU:2, one launch (start us, length us, event | category | flops | bytes accessed | tf_op | source)
XLA Modules:
  0.0 187.5 jit_solution(8741594047745029062)
XLA Ops:
  0.6 180.7 %shard_map.138 = (bf16[16,3584]{1,0:T(8,128)(2,1)}, f32[1,3,256]{2,1,0:T(4,128)}, bf16[1,256,3584]{2,1,0:T(8,128)(2,1)}, bf16[1,2,28]{2,1,0:T(2,128)(2,1)}) custom-call(bf16[16,3584]{1,0:T(8,128)(2,1)} %tok.1, s32[8,16]{1,0:T(8,128)} %bitcast.5, s32[8,16]{1,0:T(8,128)} %bitcast.6, s32[8,16]{1,0:T(8,128)} %bitcast.7, s32[64]{0:T(128)} %plan.1, ...), custom_call_target="tpu_custom_call" | custom-call | flops 6000000000 | bytes 400000000 | tf_op jit(solution)/shard_map/pallas_call | solution.py:516
  181.3 0.0 copy-start
  181.4 1.3 copy.15
  182.6 1.6 copy.19
  184.2 2.8 %copy.20 = bf16[1,256,3584]{2,1,0:T(8,128)(2,1)} copy(bf16[1,256,3584]{2,1,0:T(8,128)(2,1)} %get-tuple-element.14) | data formatting | bytes 3670016
  187.0 0.0 copy-done
  187.0 0.5 copy.21
Async XLA Ops:
  181.3 5.7 %copy-start = (bf16[1,2,28]{2,1,0:T(2,128)(2,1)S(1)}, bf16[1,2,28]{2,1,0:T(2,128)(2,1)}, u32[]{:S(2)}) copy-start(bf16[1,2,28]{2,1,0:T(2,128)(2,1)} %get-tuple-element.15) | copy-start | bytes 340

commit v3 on v2

--- a/solution.py
+++ b/solution.py
@@ -21,6 +21,8 @@
 BLOCK = 128
 CW = 256
 NCH = D // CW
+NB = 2
+NA = NCH - NB
 RB = CW // BLOCK
 F32 = jnp.float32
 BF16 = jnp.bfloat16
@@ -32,8 +34,10 @@
     comb, cnt, moved, moved_s,
     dense, mg, xs, gq, uq, dq, accg, accu, hid, ryh, ryf, crecv, zrecv, xrecv,
     pack, unpack, wslot, cntbuf, sel, sel_s, got_s, grow, urow, drow,
+    rt, bd, brc, brx, brz, bry,
     w_sem, mv_s, mv_r, xi_s, xi_r, zi_s, zi_r, ci_s, ci_r, yi_s, yi_r, m_s, m_r,
     yo_s, yo_r, co_s, co_r, zo_s, zo_r, xo_s, xo_r, n_s, n_r,
+    rt_s, rt_r, bi_s, bi_r, bo_s, bo_r,
 ):
     ep = lax.axis_index("ep")
     y = lax.axis_index("dp")
@@ -137,6 +141,42 @@
             plane = (y_dn, y_up)[k - 2] if sent else y_op
             b = xs.at[j, plane, pl.ds((k - 2) * half, half)]
         return remote(b, b, yi_s.at[j, k], yi_r.at[j, k], at_y(to))
+
+    z_gather = ((0, 1), (0, -1), (0, 2), (0, -2), (-2, 1), (2, -1), (-2, 2))
+    y_to = (y_up, y_dn, y_op)
+    y_from = (y_dn, y_up, y_op)
+
+    def b_in(i, k, sent):
+        if k < 3:
+            b, dev = bd.at[i, c, z, x, y if sent else y_from[k]], at_y(y_to[k])
+        elif k < 10:
+            off, hop = z_gather[k - 3]
+            b, dev = bd.at[i, c, zat(off if sent else off - hop), x], at_z(hop)
+        elif k < 13:
+            hop = (1, -1, 2)[k - 10]
+            b, dev = bd.at[i, c, :, xat(0 if sent else -hop)], at_x(hop)
+        else:
+            b, dev = bd.at[i, c if sent else 1 - c], other
+        return remote(b, b, bi_s.at[i, k], bi_r.at[i, k], dev)
+
+    z_scatter = ((3, 1), (-3, -1), (4, 2), (2, 2), (-2, -2), (1, 1), (-1, -1))
+
+    def b_out(i, k):
+        if k < 3:
+            src, dst, dev = bd.at[i, c, z, x, y_to[k]], bry.at[i, k], at_y(y_to[k])
+        elif k < 10:
+            off, hop = z_scatter[k - 3]
+            src, dst, dev = bd.at[i, c, zat(off), x], brz.at[i, k - 3], at_z(hop)
+        elif k < 13:
+            hop = (1, -1, 2)[k - 10]
+            src, dst, dev = bd.at[i, c, :, xat(hop)], brx.at[i, k - 10], at_x(hop)
+        else:
+            src, dst, dev = bd.at[i, 1 - c], brc.at[i], other
+        return remote(src, dst, bo_s.at[i, k], bo_r.at[i, k], dev)
+
+    def rt_copy(k, sent):
+        b = rt.at[y if sent else y_from[k]]
+        return remote(b, b, rt_s.at[k], rt_r.at[k], at_y(y_to[k]))
 
     def routing_values():
         ids = ids_t[...]
@@ -199,8 +239,11 @@
     own = c * NZ * NX + z * NX + x
     mg[own] = routing_values()
     spread_scales()
-    for j in range(NCH):
+    for j in range(NA):
         dense[j, own] = tok[:, j * CW:(j + 1) * CW]
+    for i in range(NB):
+        bd[i, c, z, x, y] = tok[:, (NA + i) * CW:(NA + i + 1) * CW]
+    rt[y] = jnp.zeros((8, PLANE), F32)
     accg[...] = jnp.zeros_like(accg)
     accu[...] = jnp.zeros_like(accu)
     pl.semaphore_wait(barrier, len(partners))
@@ -210,7 +253,10 @@
             x_start(j, k)
         return carry
 
-    lax.fori_loop(0, NCH, x_begin, 0)
+    lax.fori_loop(0, NA, x_begin, 0)
+    for i in range(NB):
+        for k in range(3):
+            b_in(i, k, True).start()
 
     def n_copy(k, sent):
         to = (y_up, y_dn, y_op)[k]
@@ -270,9 +316,34 @@
             chosen = jnp.where(spread > 0.0, 1.0, 0.0)
             unpack[i * BLOCK:(i + 1) * BLOCK, :] = chosen.astype(BF16)
             turned = jnp.transpose(spread)
-            pack[:, i * BLOCK:(i + 1) * BLOCK] = jnp.where(turned > 0.0, 1.0, 0.0).astype(BF16)
+            here = jnp.where(turned > 0.0, 1.0, 0.0)
+            at = slice(i * BLOCK, (i + 1) * BLOCK)
+            pack[y, :, at] = here.astype(BF16)
             wsum = wsum + jnp.sum(turned, axis=1, keepdims=True)
-        wslot[...] = jnp.broadcast_to(wsum, (SLOTS, BLOCK))
+            for e in range(EXP_DEV):
+                part = slice(e * CAP, (e + 1) * CAP)
+                number = here[part] * (row + 1).astype(F32)
+                rt[y, e:e + 1, at] = jnp.sum(number, axis=0, keepdims=True)
+                rt[y, EXP_DEV + e:EXP_DEV + e + 1, at] = jnp.sum(turned[part], axis=0, keepdims=True)
+        wslot[y] = jnp.broadcast_to(wsum, (SLOTS, BLOCK))
+        for k in range(3):
+            rt_copy(k, True).start()
+
+    def other_plane(k):
+        p = y_from[k]
+        rt_copy(k, False).wait_recv()
+        n = 2 * BLOCK
+        slot = (lax.broadcasted_iota(jnp.int32, (CAP, n), 0) + 1).astype(F32)
+        for e in range(EXP_DEV):
+            part = slice(e * CAP, (e + 1) * CAP)
+            wsum = jnp.zeros((CAP, 1), F32)
+            for i in range(PLANE // n):
+                at = slice(i * n, (i + 1) * n)
+                here = slot == rt[p, e:e + 1, at]
+                pack[p, part, at] = jnp.where(here, 1.0, 0.0).astype(BF16)
+                weights = jnp.where(here, rt[p, EXP_DEV + e:EXP_DEV + e + 1, at], 0.0)
+                wsum = wsum + jnp.sum(weights, axis=1, keepdims=True)
+            wslot[p, part] = jnp.broadcast_to(wsum, (CAP, BLOCK))
 
     def weight(q, e, j, s):
         parts = []
@@ -282,17 +353,17 @@
             parts.append((rows.astype(F32) * row).astype(BF16))
         return jnp.concatenate(parts, axis=0)
 
-    def stage(t, late, fn):
+    def stage(t, late, fn, n=NA):
         j = t - late
 
-        @pl.when((j >= 0) & (j < NCH))
+        @pl.when((j >= 0) & (j < n))
         def _():
             fn(j)
 
     def i1(j):
         for k in range(3):
             x_recv(j, k)
-        for k in range(4):
+        for k in (2, 3, 0, 1):
             z_start(j, k)
 
     def i2(j):
@@ -315,7 +386,7 @@
             routes()
 
         full = dense[j].reshape(PLANE, CW)
-        xs[j, y] = jnp.dot(pack[...], full, preferred_element_type=F32).astype(BF16)
+        xs[j, y] = jnp.dot(pack[y], full, preferred_element_type=F32).astype(BF16)
         g_y(j, 0, True).start()
         g_y(j, 1, True).start()
 
@@ -325,6 +396,12 @@
         g_y(j, 1, False).wait_recv()
         g_y(j, 3, True).start()
 
+    def first_layer(j):
+        for e in range(EXP_DEV):
+            rows = xs[j, :, e * CAP:(e + 1) * CAP, :].reshape(NY * CAP, CW)
+            accg[e] += jnp.dot(rows, weight(gq, e, j, grow), preferred_element_type=F32)
+            accu[e] += jnp.dot(rows, weight(uq, e, j, urow), preferred_element_type=F32)
+
     def i9(j):
         @pl.when(j == 0)
         def _():
@@ -333,10 +410,37 @@
 
         g_y(j, 2, False).wait_recv()
         g_y(j, 3, False).wait_recv()
-        for e in range(EXP_DEV):
-            rows = xs[j, :, e * CAP:(e + 1) * CAP, :].reshape(NY * CAP, CW)
-            accg[e] += jnp.dot(rows, weight(gq, e, j, grow), preferred_element_type=F32)
-            accu[e] += jnp.dot(rows, weight(uq, e, j, urow), preferred_element_type=F32)
+        first_layer(j)
+
+    def b1(i):
+        for k in range(3):
+            b_in(i, k, False).wait_recv()
+        for k in (5, 6, 3, 4):
+            b_in(i, k, True).start()
+
+    def b2(i):
+        b_in(i, 5, False).wait_recv()
+        b_in(i, 6, False).wait_recv()
+        for k in (9, 7, 8):
+            b_in(i, k, True).start()
+
+    def b3(i):
+        for k in (3, 4, 7, 8, 9):
+            b_in(i, k, False).wait_recv()
+        for k in (10, 11, 12):
+            b_in(i, k, True).start()
+
+    def b4(i):
+        for k in (10, 11, 12):
+            b_in(i, k, False).wait_recv()
+        b_in(i, 13, True).start()
+
+    def b5(i):
+        b_in(i, 13, False).wait_recv()
+        for p in range(NY):
+            rows = bd[i, :, :, :, p].reshape(PLANE, CW)
+            xs[NA + i, p] = jnp.dot(pack[p], rows, preferred_element_type=F32).astype(BF16)
+        first_layer(NA + i)
 
     def in_tick(t, carry):
         stage(t, 5, i7)
@@ -344,7 +448,7 @@
         stage(t, 2, i2)
         stage(t, 0, i1)
 
-        @pl.when(t == 6)
+        @pl.when(t == 1)
         def _():
             select_moved()
 
@@ -352,12 +456,24 @@
         def _():
             fill_slots()
 
-        stage(t, 6, lambda j: mv(j).start())
+        @pl.when((t >= 1) & (t < 8))
+        def _():
+            mv(2 * t - 2).start()
+            mv(2 * t - 1).start()
+
         stage(t, 7, i8)
         stage(t, 9, i9)
+        stage(t, 10, lambda _: other_plane(0), 1)
+        stage(t, 11, lambda _: other_plane(1), 1)
+        stage(t, 12, lambda _: other_plane(2), 1)
+        stage(t, 3, b1, NB)
+        stage(t, 5, b2, NB)
+        stage(t, 7, b3, NB)
+        stage(t, 15, b4, NB)
+        stage(t, 16, b5, NB)
         return carry
 
-    lax.fori_loop(0, NCH + 9, in_tick, 0)
+    lax.fori_loop(0, NA + 9, in_tick, 0)
 
     for e in range(EXP_DEV):
         v = accg[e]
@@ -373,7 +489,14 @@
             g_y(j, k, True).wait_send()
         return carry
 
-    lax.fori_loop(0, NCH, in_done, 0)
+    lax.fori_loop(0, NA, in_done, 0)
+
+    def b_in_done(i, carry):
+        for k in range(14):
+            b_in(i, k, True).wait_send()
+        return carry
+
+    lax.fori_loop(0, NB, b_in_done, 0)
     for k in range(3):
         n_copy(k, False).wait_recv()
     total = (cntbuf[0] + cntbuf[1] + cntbuf[2] + cntbuf[3]) * (1.0 / MOST)
@@ -413,7 +536,7 @@
         at = pl.ds(c * NZ * NX + zat(off - hop) * NX, NX)
         dense[j, at] = add(dense[j, at], zrecv[j, k])
 
-    def o0(j):
+    def second_layer(j):
         cols = pl.ds(pl.multiple_of(j * CW, CW), CW)
         for e in range(EXP_DEV):
             parts = []
@@ -424,6 +547,9 @@
             w = jnp.concatenate(parts, axis=0)
             out = jnp.dot(hid[e], w, preferred_element_type=F32).astype(BF16)
             xs[j, :, e * CAP:(e + 1) * CAP, :] = out.reshape(NY, CAP, CW)
+
+    def o0(j):
+        second_layer(j)
         o_y(j, 0, True).start()
         o_y(j, 1, True).start()
 
@@ -439,7 +565,7 @@
         o_y(j, 2, False).wait_recv()
         o_y(j, 3, False).wait_recv()
         total = xs[j, y].astype(F32) + ryf[j, 0].astype(F32) + ryf[j, 1].astype(F32)
-        scaled = (total * wslot[:, 0:1]).astype(BF16)
+        scaled = (total * wslot[y, :, 0:1]).astype(BF16)
         n = 256
         for i in range(PLANE // n):
             out = jnp.dot(unpack[i * n:(i + 1) * n, :], scaled, preferred_element_type=F32)
@@ -477,6 +603,62 @@
             total = total + xrecv[j, k].astype(F32)
         comb[:, pl.ds(pl.multiple_of(j * CW, CW), CW)] = total.astype(BF16)
 
+    def c0(i):
+        second_layer(NA + i)
+        n = 2 * BLOCK
+        for p in range(NY):
+            scaled = (xs[NA + i, p].astype(F32) * wslot[p, :, 0:1]).astype(BF16)
+            for h in range(NC):
+                half_rows = pack[p, :, h * (PLANE // NC):(h + 1) * (PLANE // NC)]
+                out = lax.dot_general(
+                    half_rows, scaled, (((0,), (0,)), ((), ())), preferred_element_type=F32
+                )
+                bd[i, h, :, :, p] = out.astype(BF16).reshape(NZ, NX, ROWS, CW)
+        b_out(i, 13).start()
+
+    def c1(i):
+        b_out(i, 13).wait_recv()
+        for zz in range(NZ):
+            bd[i, c, zz] = add(bd[i, c, zz], brc[i, zz])
+        for k in (10, 11, 12):
+            b_out(i, k).start()
+
+    def c2(i):
+        for k in (10, 11, 12):
+            b_out(i, k).wait_recv()
+        for zz in range(NZ):
+            total = bd[i, c, zz, x].astype(F32)
+            for k in range(3):
+                total = total + brx[i, k, zz].astype(F32)
+            bd[i, c, zz, x] = total.astype(BF16)
+        for k in (5, 3, 4, 8, 9):
+            b_out(i, k).start()
+
+    def c3(i):
+        for k in range(3):
+            off, hop = z_scatter[k]
+            b_out(i, 3 + k).wait_recv()
+            zz = zat(off - hop)
+            bd[i, c, zz, x] = add(bd[i, c, zz, x], brz[i, k])
+        b_out(i, 6).start()
+        b_out(i, 7).start()
+
+    def c4(i):
+        total = bd[i, c, z, x].astype(F32)
+        for k in range(3, 7):
+            b_out(i, 3 + k).wait_recv()
+            total = total + brz[i, k].astype(F32)
+        bd[i, c, z, x] = total.astype(BF16)
+        for k in range(3):
+            b_out(i, k).start()
+
+    def c5(i):
+        total = bd[i, c, z, x, y].astype(F32)
+        for k in range(3):
+            b_out(i, k).wait_recv()
+            total = total + bry[i, k].astype(F32)
+        comb[:, pl.ds(pl.multiple_of((NA + i) * CW, CW), CW)] = total.astype(BF16)
+
     def out_tick(t, carry):
         stage(t, 0, o0)
         stage(t, 2, o1)
@@ -485,9 +667,17 @@
         stage(t, 9, o5)
         stage(t, 11, o6)
         stage(t, 4, o2)
+
+
+        stage(t, 1, c0, NB)
+        stage(t, 3, c1, NB)
+        stage(t, 10, c2, NB)
+        stage(t, 13, c3, NB)
+        stage(t, 15, c4, NB)
+        stage(t, 18, c5, NB)
         return carry
 
-    lax.fori_loop(0, NCH + 11, out_tick, 0)
+    lax.fori_loop(0, NA + 11, out_tick, 0)
 
     def out_done(j, carry):
         for k in range(4):
@@ -499,7 +689,16 @@
             o_x(j, k).wait_send()
         return carry
 
-    lax.fori_loop(0, NCH, out_done, 0)
+    lax.fori_loop(0, NA, out_done, 0)
+
+    def b_out_done(i, carry):
+        for k in range(14):
+            b_out(i, k).wait_send()
+        return carry
+
+    lax.fori_loop(0, NB, b_out_done, 0)
+    for k in range(3):
+        rt_copy(k, True).wait_send()
     for k in range(3):
         n_copy(k, True).wait_send()
     mv(None).wait()
@@ -524,7 +723,7 @@
         in_specs=[vmem] * 4 + [smem] + [vmem] * 3 + [hbm] * 3,
         out_specs=(vmem, vmem, hbm, vmem),
         scratch_shapes=[
-            pltpu.VMEM((NCH, blocks, ROWS, CW), BF16),
+            pltpu.VMEM((NA, blocks, ROWS, CW), BF16),
             pltpu.VMEM((blocks, ROWS, BLOCK), BF16),
             pltpu.VMEM((NCH, NY, SLOTS, CW), BF16),
             pltpu.VMEM((EXP_DEV, D, FF), BF16),
@@ -533,14 +732,14 @@
             pltpu.VMEM((EXP_DEV, NY * CAP, FF), F32),
             pltpu.VMEM((EXP_DEV, NY * CAP, FF), F32),
             pltpu.VMEM((EXP_DEV, NY * CAP, FF), BF16),
-            pltpu.VMEM((NCH, 2, SLOTS // 2, CW), BF16),
-            pltpu.VMEM((NCH, 2, SLOTS, CW), BF16),
-            pltpu.VMEM((NCH, blocks // 2, ROWS, CW), BF16),
-            pltpu.VMEM((NCH, 7, NX, ROWS, CW), BF16),
-            pltpu.VMEM((NCH, 3, ROWS, CW), BF16),
-            pltpu.VMEM((SLOTS, PLANE), BF16),
+            pltpu.VMEM((NA, 2, SLOTS // 2, CW), BF16),
+            pltpu.VMEM((NA, 2, SLOTS, CW), BF16),
+            pltpu.VMEM((NA, blocks // 2, ROWS, CW), BF16),
+            pltpu.VMEM((NA, 7, NX, ROWS, CW), BF16),
+            pltpu.VMEM((NA, 3, ROWS, CW), BF16),
+            pltpu.VMEM((NY, SLOTS, PLANE), BF16),
             pltpu.VMEM((PLANE, SLOTS), BF16),
-            pltpu.VMEM((SLOTS, BLOCK), F32),
+            pltpu.VMEM((NY, SLOTS, BLOCK), F32),
             pltpu.VMEM((NY, 8, N_EP * NY), F32),
             pltpu.VMEM((FF, D), BF16),
             pltpu.VMEM((ROWS, BLOCK), BF16),
@@ -548,18 +747,27 @@
             pltpu.VMEM((EXP_DEV, D // BLOCK, FF), F32),
             pltpu.VMEM((EXP_DEV, D // BLOCK, FF), F32),
             pltpu.VMEM((EXP_DEV, FF // BLOCK, D), F32),
+            pltpu.VMEM((NY, 8, PLANE), F32),
+            pltpu.VMEM((NB, NC, NZ, NX, NY, ROWS, CW), BF16),
+            pltpu.VMEM((NB, NZ, NX, NY, ROWS, CW), BF16),
+            pltpu.VMEM((NB, 3, NZ, NY, ROWS, CW), BF16),
+            pltpu.VMEM((NB, 7, NY, ROWS, CW), BF16),
+            pltpu.VMEM((NB, 3, ROWS, CW), BF16),
             dma((3,)),
             dma((2,)), dma((2,)),
-            dma((NCH, 3)), dma((NCH, 3)),
-            dma((NCH, 7)), dma((NCH, 7)),
-            dma((NCH,)), dma((NCH,)),
-            dma((NCH, 4)), dma((NCH, 4)),
+            dma((NA, 3)), dma((NA, 3)),
+            dma((NA, 7)), dma((NA, 7)),
+            dma((NA,)), dma((NA,)),
+            dma((NA, 4)), dma((NA, 4)),
             dma((11,)), dma((11,)),
-            dma((NCH, 4)), dma((NCH, 4)),
-            dma((NCH,)), dma((NCH,)),
-            dma((NCH, 7)), dma((NCH, 7)),
-            dma((NCH, 3)), dma((NCH, 3)),
+            dma((NA, 4)), dma((NA, 4)),
+            dma((NA,)), dma((NA,)),
+            dma((NA, 7)), dma((NA, 7)),
+            dma((NA, 3)), dma((NA, 3)),
             dma((3,)), dma((3,)),
+            dma((3,)), dma((3,)),
+            dma((NB, 14)), dma((NB, 14)),
+            dma((NB, 14)), dma((NB, 14)),
         ],
         compiler_params=pltpu.CompilerParams(
             collective_id=0, has_side_effects=True, vmem_limit_bytes=60 * 1024 * 1024

time: 189 us -> 178 us (0.942)
  Pallas kernels: 181 us -> 170 us
    pallas_call x1, Pallas kernels: 181 us -> 170 us  [layer(): pl.pallas_call(kernel, out_shape=(jax.ShapeDtypeStruct((ROWS, D), BF16),...]
where the time goes in v3:
time: 178 us; the launch traced here: 177 us
  Pallas kernels  170 us (96%)
  local copies, waits for them, and re-layouts  6.17 us (3%)
    pallas_call x1, Pallas kernels, layer(): pl.pallas_call(kernel, out_shape=(jax.ShapeDtypeStruct((ROWS, D), BF16),...  170 us
    unnamed x5, local copies, waits for them, and re-layouts  4.91 us

profile of v3, /device:TPU:2, one launch (start us, length us, event | category | flops | bytes accessed | tf_op | source)
XLA Modules:
  0.0 177.2 jit_solution(18205213634084113389)
XLA Ops:
  0.6 170.4 %shard_map.138 = (bf16[16,3584]{1,0:T(8,128)(2,1)}, f32[1,3,256]{2,1,0:T(4,128)}, bf16[1,256,3584]{2,1,0:T(8,128)(2,1)}, bf16[1,2,28]{2,1,0:T(2,128)(2,1)}) custom-call(bf16[16,3584]{1,0:T(8,128)(2,1)} %tok.1, s32[8,16]{1,0:T(8,128)} %bitcast.5, s32[8,16]{1,0:T(8,128)} %bitcast.6, s32[8,16]{1,0:T(8,128)} %bitcast.7, s32[64]{0:T(128)} %plan.1, ...), custom_call_target="tpu_custom_call" | custom-call | flops 6000000000 | bytes 400000000 | tf_op jit(solution)/shard_map/pallas_call | solution.py:715
  171.0 0.0 copy-start
  171.0 1.3 copy.15
  172.3 1.6 copy.19
  173.8 2.8 %copy.20 = bf16[1,256,3584]{2,1,0:T(8,128)(2,1)} copy(bf16[1,256,3584]{2,1,0:T(8,128)(2,1)} %get-tuple-element.14) | data formatting | bytes 3670016
  176.7 0.0 copy-done
  176.7 0.5 copy.21
Async XLA Ops:
  171.0 5.7 %copy-start = (bf16[1,2,28]{2,1,0:T(2,128)(2,1)S(1)}, bf16[1,2,28]{2,1,0:T(2,128)(2,1)}, u32[]{:S(2)}) copy-start(bf16[1,2,28]{2,1,0:T(2,128)(2,1)} %get-tuple-element.15) | copy-start | bytes 340

commit v4 on v3

--- a/solution.py
+++ b/solution.py
@@ -34,7 +34,7 @@
     comb, cnt, moved, moved_s,
     dense, mg, xs, gq, uq, dq, accg, accu, hid, ryh, ryf, crecv, zrecv, xrecv,
     pack, unpack, wslot, cntbuf, sel, sel_s, got_s, grow, urow, drow,
-    rt, bd, brc, brx, brz, bry,
+    rt, shares, bd, brc, brx, brz, bry,
     w_sem, mv_s, mv_r, xi_s, xi_r, zi_s, zi_r, ci_s, ci_r, yi_s, yi_r, m_s, m_r,
     yo_s, yo_r, co_s, co_r, zo_s, zo_r, xo_s, xo_r, n_s, n_r,
     rt_s, rt_r, bi_s, bi_r, bo_s, bo_r,
@@ -293,7 +293,6 @@
         before = (lane < row).astype(BF16)
         first = (ep * EXP_DEV).astype(F32)
         sofar = jnp.zeros((1, BLOCK), F32)
-        wsum = jnp.zeros((SLOTS, 1), F32)
         for i in range(PLANE // BLOCK):
             m = rows_of(i)
             gates = pltpu.roll(m, BLOCK - TOPK, 1)
@@ -316,16 +315,23 @@
             chosen = jnp.where(spread > 0.0, 1.0, 0.0)
             unpack[i * BLOCK:(i + 1) * BLOCK, :] = chosen.astype(BF16)
             turned = jnp.transpose(spread)
-            here = jnp.where(turned > 0.0, 1.0, 0.0)
             at = slice(i * BLOCK, (i + 1) * BLOCK)
-            pack[y, :, at] = here.astype(BF16)
-            wsum = wsum + jnp.sum(turned, axis=1, keepdims=True)
-            for e in range(EXP_DEV):
-                part = slice(e * CAP, (e + 1) * CAP)
-                number = here[part] * (row + 1).astype(F32)
+            shares[:, at] = turned
+            pack[y, :, at] = jnp.where(turned > 0.0, 1.0, 0.0).astype(BF16)
+
+    def send_routes():
+        row = lax.broadcasted_iota(jnp.int32, (CAP, BLOCK), 0)
+        for e in range(EXP_DEV):
+            part = slice(e * CAP, (e + 1) * CAP)
+            wsum = jnp.zeros((CAP, 1), F32)
+            for i in range(PLANE // BLOCK):
+                at = slice(i * BLOCK, (i + 1) * BLOCK)
+                turned = shares[part, at]
+                number = jnp.where(turned > 0.0, (row + 1).astype(F32), 0.0)
+                wsum = wsum + jnp.sum(turned, axis=1, keepdims=True)
                 rt[y, e:e + 1, at] = jnp.sum(number, axis=0, keepdims=True)
-                rt[y, EXP_DEV + e:EXP_DEV + e + 1, at] = jnp.sum(turned[part], axis=0, keepdims=True)
-        wslot[y] = jnp.broadcast_to(wsum, (SLOTS, BLOCK))
+                rt[y, EXP_DEV + e:EXP_DEV + e + 1, at] = jnp.sum(turned, axis=0, keepdims=True)
+            wslot[y, part] = jnp.broadcast_to(wsum, (CAP, BLOCK))
         for k in range(3):
             rt_copy(k, True).start()
 
@@ -452,20 +458,22 @@
         def _():
             select_moved()
 
+        @pl.when((t >= 1) & (t < 8))
+        def _():
+            mv(t - 1).start()
+
+        @pl.when(t == 7)
+        def _():
+            send_routes()
+
         @pl.when(t == 8)
         def _():
             fill_slots()
-
-        @pl.when((t >= 1) & (t < 8))
-        def _():
-            mv(2 * t - 2).start()
-            mv(2 * t - 1).start()
 
         stage(t, 7, i8)
         stage(t, 9, i9)
-        stage(t, 10, lambda _: other_plane(0), 1)
-        stage(t, 11, lambda _: other_plane(1), 1)
-        stage(t, 12, lambda _: other_plane(2), 1)
+        for k in range(3):
+            stage(t, 10 + k, lambda _, k=k: other_plane(k), 1)
         stage(t, 3, b1, NB)
         stage(t, 5, b2, NB)
         stage(t, 7, b3, NB)
@@ -500,7 +508,8 @@
     for k in range(3):
         n_copy(k, False).wait_recv()
     total = (cntbuf[0] + cntbuf[1] + cntbuf[2] + cntbuf[3]) * (1.0 / MOST)
-    cnt[0] = total[0:EXP_DEV + 1]
+    for k in range(EXP_DEV + 1):
+        cnt[k] = total[k:k + 1]
 
     def o_y(j, k, sent):
         to = (y_up, y_dn)[k % 2]
@@ -659,6 +668,13 @@
             total = total + bry[i, k].astype(F32)
         comb[:, pl.ds(pl.multiple_of((NA + i) * CW, CW), CW)] = total.astype(BF16)
 
+    def spaced(t, late, fn):
+        i = (t - late) // 3
+
+        @pl.when((t >= late) & (t < late + 3 * NB) & ((t - late) % 3 == 0))
+        def _():
+            fn(i)
+
     def out_tick(t, carry):
         stage(t, 0, o0)
         stage(t, 2, o1)
@@ -668,13 +684,16 @@
         stage(t, 11, o6)
         stage(t, 4, o2)
 
-
-        stage(t, 1, c0, NB)
-        stage(t, 3, c1, NB)
-        stage(t, 10, c2, NB)
-        stage(t, 13, c3, NB)
-        stage(t, 15, c4, NB)
-        stage(t, 18, c5, NB)
+        @pl.when((t >= 8) & (t < 15))
+        def _():
+            mv(t - 1).start()
+
+        spaced(t, 1, c0)
+        spaced(t, 2, c1)
+        spaced(t, 9, c2)
+        spaced(t, 12, c3)
+        spaced(t, 14, c4)
+        spaced(t, 17, c5)
         return carry
 
     lax.fori_loop(0, NA + 11, out_tick, 0)
@@ -716,7 +735,7 @@
         kernel,
         out_shape=(
             jax.ShapeDtypeStruct((ROWS, D), BF16),
-            jax.ShapeDtypeStruct((1, EXP_DEV + 1, N_EP * NY), F32),
+            jax.ShapeDtypeStruct((EXP_DEV + 1, 1, N_EP * NY), F32),
             jax.ShapeDtypeStruct((1, FF, D), BF16),
             jax.ShapeDtypeStruct((1, FF // BLOCK, D // BLOCK), BF16),
         ),
@@ -748,6 +767,7 @@
             pltpu.VMEM((EXP_DEV, D // BLOCK, FF), F32),
             pltpu.VMEM((EXP_DEV, FF // BLOCK, D), F32),
             pltpu.VMEM((NY, 8, PLANE), F32),
+            pltpu.VMEM((SLOTS, PLANE), F32),
             pltpu.VMEM((NB, NC, NZ, NX, NY, ROWS, CW), BF16),
             pltpu.VMEM((NB, NZ, NX, NY, ROWS, CW), BF16),
             pltpu.VMEM((NB, 3, NZ, NY, ROWS, CW), BF16),
@@ -782,11 +802,12 @@
     tokens, top_ids, gate_int, replica_pick, plan,
     gate_q, gate_scale, up_q, up_scale, down_q, down_scale,
 ):
-    return layer(
+    combined, fill, moved, moved_scale = layer(
         tokens, top_ids.T, gate_int.T, replica_pick.T, plan,
         gate_scale.transpose(0, 2, 1), up_scale.transpose(0, 2, 1), down_scale,
         gate_q, up_q, down_q,
     )
+    return combined, fill.transpose(1, 0, 2), moved, moved_scale
 
 
 def solution(mesh):

time: 178 us -> 178 us (level)
    unnamed x5 -> x6, local copies, waits for them, and re-layouts: 4.91 us -> 6.16 us
where the time goes in v4:
time: 178 us; the launch traced here: 176 us
  Pallas kernels  169 us (95%)
  local copies, waits for them, and re-layouts  6.16 us (3%)
    pallas_call x1, Pallas kernels, layer(): pl.pallas_call(kernel, out_shape=(jax.ShapeDtypeStruct((ROWS, D), BF16),...  169 us
    unnamed x6, local copies, waits for them, and re-layouts  6.16 us

profile of v4, /device:TPU:2, one launch (start us, length us, event | category | flops | bytes accessed | tf_op | source)
XLA Modules:
  0.0 176.3 jit_solution(6733703340357657600)
XLA Ops:
  0.6 169.5 %shard_map.138 = (bf16[16,3584]{1,0:T(8,128)(2,1)}, f32[3,1,256]{2,1,0:T(1,128)}, bf16[1,256,3584]{2,1,0:T(8,128)(2,1)}, bf16[1,2,28]{2,1,0:T(2,128)(2,1)}) custom-call(bf16[16,3584]{1,0:T(8,128)(2,1)} %tok.1, s32[8,16]{1,0:T(8,128)} %bitcast.7, s32[8,16]{1,0:T(8,128)} %bitcast.8, s32[8,16]{1,0:T(8,128)} %bitcast.9, s32[64]{0:T(128)} %plan.1, ...), custom_call_target="tpu_custom_call" | custom-call | flops 6000000000 | bytes 400000000 | tf_op jit(solution)/shard_map/pallas_call | solution.py:734
  170.1 0.0 copy-start
  170.1 1.6 copy.19
  171.7 1.2 copy.20
  172.9 2.8 %copy.21 = bf16[1,256,3584]{2,1,0:T(8,128)(2,1)} copy(bf16[1,256,3584]{2,1,0:T(8,128)(2,1)} %get-tuple-element.18) | data formatting | bytes 3670016
  175.8 0.0 copy-done
  175.8 0.5 copy.22
Async XLA Ops:
  170.1 5.7 %copy-start = (bf16[1,2,28]{2,1,0:T(2,128)(2,1)S(1)}, bf16[1,2,28]{2,1,0:T(2,128)(2,1)}, u32[]{:S(2)}) copy-start(bf16[1,2,28]{2,1,0:T(2,128)(2,1)} %get-tuple-element.19) | copy-start | bytes 340
